TPU v7x, 32 devices: a whole 2x2x4 slice. The times are simulated.
32 devices in a mesh: slab: 2 (over y), gx: 4 (over z), gy: 4 (over x, core).
Axes of the slice: x: 2, y: 2, z: 4, core: 2. Of those that a mesh axis runs over, the one named last changes fastest.
Arguments:
- charge: float32 [32, 512, 512], P(None, ('slab', 'gx'), 'gy'), parts along dimension 1, may hold values from -6 to 6
- surface_charge: float32 [2, 512, 512], P(None, ('slab', 'gx'), 'gy'), parts along dimension 1, may hold values from -6 to 6
Outputs:
- potential: float32 [32, 512, 512], P(None, ('slab', 'gx'), 'gy'), parts along dimension 1
- interface_residual: float32 [32, 512, 512], P(None, ('slab', 'gx'), 'gy'), parts along dimension 1
There are 2 independent parts, one for each index of `slab`. A program takes and returns all parts, laid end to end along the dimension named above; each array names one. Nothing has to cross between parts.
All inputs are finite; a program needn't handle non-finite values.
Results may differ from a plain program's by a relative error of at most 0.0003.
Values sent between devices are 32-bit elements; how exact they have to be, the bound alone decides.
A program may use at most 64 MiB of HBM per device.

v0:
```python
import functools

import jax
import jax.numpy as jnp
import ml_dtypes
import numpy as np
from jax import lax
from jax.experimental import pallas as pl
from jax.experimental.pallas import tpu as pltpu
from jax.sharding import PartitionSpec as P

ITERS = 2


SCREEN = 0.02


def padded(block, sides, width):
    for axis, dim in sides:
        count = lax.axis_size(axis)
        forward = [(i, i + 1) for i in range(count - 1)]
        forward.append((count - 1, 0))
        backward = [(target, source) for source, target in forward]
        low = lax.ppermute(
            lax.slice_in_dim(block, block.shape[dim] - width, None, axis=dim), axis, forward
        )
        high = lax.ppermute(lax.slice_in_dim(block, 0, width, axis=dim), axis, backward)
        block = jnp.concatenate([low, block, high], axis=dim)
    return block


def sine_full(count):
    index = jnp.arange(count).astype(jnp.float32)
    return jnp.sqrt(2.0 / count) * jnp.sin(jnp.pi * jnp.outer(index, index) / count)


def cosine_table(count):
    place = jnp.arange(count).astype(jnp.float32) + 0.5
    order = jnp.arange(count).astype(jnp.float32)
    factor = jnp.where(order == 0.0, jnp.sqrt(1.0 / count), jnp.sqrt(2.0 / count))
    return factor[None, :] * jnp.cos(jnp.pi * jnp.outer(place, order) / count)


def spectrum_table(depth, width, height):
    across = 2.0 - 2.0 * jnp.cos(jnp.pi * jnp.arange(width).astype(jnp.float32) / width)
    along = 2.0 - 2.0 * jnp.cos(jnp.pi * jnp.arange(height).astype(jnp.float32) / height)
    vertical = 2.0 - 2.0 * jnp.cos(jnp.pi * jnp.arange(depth).astype(jnp.float32) / depth)
    return SCREEN + vertical[:, None, None] + across[None, :, None] + along[None, None, :]


def apply_full(field):
    row_rims = jnp.stack([field[:, 0, :], field[:, -1, :]], 1)
    row_ext = padded(row_rims, (("gx", 1),), 1)
    col_rims = jnp.stack([field[:, :, 0], field[:, :, -1]], 0)
    col_ext = padded(col_rims, (("gy", 0),), 1)
    from_below_x = jnp.concatenate([row_ext[:, 0:1, :], field[:, :-1, :]], 1)
    from_above_x = jnp.concatenate([field[:, 1:, :], row_ext[:, 3:4, :]], 1)
    from_below_y = jnp.concatenate([col_ext[0][:, :, None], field[:, :, :-1]], 2)
    from_above_y = jnp.concatenate([field[:, :, 1:], col_ext[3][:, :, None]], 2)
    beside = from_below_x + from_above_x + from_below_y + from_above_y
    upper = jnp.concatenate([field[1:], field[-1:]], 0)
    lower = jnp.concatenate([field[:1], field[:-1]], 0)
    return (6.0 + SCREEN) * field - beside - upper - lower


def solve_interior(field, sines_x, sines_y, cosines, spectrum):
    high = lax.Precision.HIGHEST
    depth, width, height = field.shape
    hat = jnp.dot(field.reshape(depth * width, height), sines_y, precision=high).reshape(
        depth, width, height
    )
    hat = jnp.matmul(sines_x, hat, precision=high)
    hat = jnp.dot(cosines.T, hat.reshape(depth, width * height), precision=high).reshape(
        depth, width, height
    )
    hat = hat / spectrum
    back = jnp.dot(cosines, hat.reshape(depth, width * height), precision=high).reshape(
        depth, width, height
    )
    back = jnp.matmul(sines_x, back, precision=high)
    back = jnp.dot(back.reshape(depth * width, height), sines_y, precision=high)
    return back.reshape(depth, width, height)


def norm_total(residual):
    return lax.psum(jnp.sum(residual * residual), ("gx", "gy"))


def curvature_total(direction, image):
    return lax.psum(jnp.sum(direction * image), ("gx", "gy"))


def on_device(charge, surface_charge):
    depth, width, height = charge.shape
    sines_x = sine_full(width)
    sines_y = sine_full(height)
    cosines = cosine_table(depth)
    spectrum = spectrum_table(depth, width, height)
    row_place = lax.broadcasted_iota(jnp.int32, (1, width, height), 1)
    col_place = lax.broadcasted_iota(jnp.int32, (1, width, height), 2)
    gamma = jnp.where((row_place == 0) | (col_place == 0), 1.0, 0.0).astype(jnp.float32)
    source = charge.at[0].add(surface_charge[0]).at[-1].add(surface_charge[1])
    base = solve_interior(source, sines_x, sines_y, cosines, spectrum)
    reduced = gamma * (source - apply_full(base))
    iterate = jnp.zeros_like(reduced)
    residual = reduced
    direction = reduced
    norm_now = norm_total(residual)
    for step in range(ITERS):
        lifted = -solve_interior(apply_full(direction), sines_x, sines_y, cosines, spectrum)
        image, lifted = (gamma * apply_full(direction + lifted), lifted)
        alpha = norm_now / curvature_total(direction, image)
        iterate = iterate + alpha * direction
        residual = residual - alpha * image
        if step + 1 < ITERS:
            norm_next = norm_total(residual)
            direction = residual + norm_next / norm_now * direction
            norm_now = norm_next
    correction = -solve_interior(apply_full(iterate), sines_x, sines_y, cosines, spectrum)
    potential = iterate + base + correction
    return (potential, residual)


DEPTH, WIDTH, HEIGHT = 32, 64, 128
F32, BF16 = jnp.float32, jnp.bfloat16


def halves(table):
    table = np.asarray(table, np.float64)
    high = table.astype(np.float32).astype(ml_dtypes.bfloat16)
    low = (table - high.astype(np.float64)).astype(np.float32).astype(ml_dtypes.bfloat16)
    return high, low


def sine_unit(count):
    index = np.arange(count)
    table = np.sqrt(2.0 / count) * np.sin(np.pi * np.outer(index, index) / count)
    table[0, 0] = 1.0
    return table


def host_tables():
    place, order = np.arange(DEPTH) + 0.5, np.arange(DEPTH)
    factor = np.where(order == 0, np.sqrt(1.0 / DEPTH), np.sqrt(2.0 / DEPTH))
    cosines = factor[None, :] * np.cos(np.pi * np.outer(place, order) / DEPTH)
    sin_x, sin_y = sine_unit(WIDTH), sine_unit(HEIGHT)
    vertical = 2.0 - 2.0 * np.cos(np.pi * order / DEPTH)
    across = 2.0 - 2.0 * np.cos(np.pi * np.arange(WIDTH) / WIDTH)
    along = 2.0 - 2.0 * np.cos(np.pi * np.arange(HEIGHT) / HEIGHT)
    ux = np.sqrt(2.0 / WIDTH) * np.sin(np.pi * np.arange(WIDTH) / WIDTH)
    uy = np.sqrt(2.0 / HEIGHT) * np.sin(np.pi * np.arange(HEIGHT) / HEIGHT)
    sx = np.where(np.arange(WIDTH) % 2 == 1, 1.0, -1.0)
    sy = np.where(np.arange(HEIGHT) % 2 == 1, 1.0, -1.0)
    sx[0] = sy[0] = 0.0
    ex, ey = np.eye(WIDTH)[0], np.eye(HEIGHT)[0]
    t = {}
    t["zf"] = halves(np.kron(cosines.T, np.eye(8)))
    t["zi"] = halves(np.kron(cosines, np.eye(8)))
    t["x"] = halves(np.kron(np.eye(4), sin_x))
    t["y"] = halves(sin_y)
    plane = SCREEN + across[:, None] + along[None, :]
    t["plane"] = plane.astype(np.float32)
    t["vert"] = [float(v) for v in vertical]
    t["ur"] = halves(np.concatenate([np.kron(np.eye(4), (ux + ex)[None]), np.kron(np.eye(4), (ux * sx)[None])], 0))
    uc = np.zeros((16, HEIGHT))
    uc[0], uc[1], uc[2] = uy + ey, uy * sy, ey
    t["uc"] = halves(uc)
    spec = plane[None] + vertical[:, None, None]
    inner = np.zeros((WIDTH, HEIGHT))
    inner[1:, 1:] = 1.0
    inv = inner / spec
    row_near = np.einsum("a,kab->kb", ux * ux, inv)
    row_far = np.einsum("a,kab->kb", ux * ux * sx, inv)
    col_near = np.einsum("b,kab->ka", uy * uy, inv)
    col_far = np.einsum("b,kab->ka", uy * uy * sy, inv)
    row_coef = SCREEN + vertical[:, None] + 2.0 + along[None, :] - 2.0 * row_near
    col_coef = SCREEN + vertical[:, None] + 2.0 + across[None, :] - 2.0 * col_near
    row_coef[:, 0] = SCREEN + vertical + 4.0
    col_coef[:, 0] = 0.0
    own = np.zeros((DEPTH // 2, 8, HEIGHT))
    own[:, 0], own[:, 1] = row_coef[0::2], row_coef[1::2]
    own[:, 2], own[:, 3] = row_far[0::2], row_far[1::2]
    own[:, 4] = np.concatenate([col_coef[0::2], col_coef[1::2]], 1)
    own[:, 5] = np.concatenate([col_far[0::2], col_far[1::2]], 1)
    own[:, 6], own[:, 7] = vertical[0::2, None], vertical[1::2, None]
    t["own"] = own.astype(np.float32)
    border = np.zeros((WIDTH, HEIGHT))
    border[0], border[:, 0] = uy, ux
    t["pair"] = np.stack([np.outer(ux, uy), border]).astype(np.float32)
    signs = np.zeros((8, HEIGHT))
    signs[0] = sy
    signs[1] = np.concatenate([sx, sx])
    t["signs"] = signs.astype(np.float32)
    zero = np.zeros(WIDTH)
    left = np.zeros((8, HEIGHT))
    left[0], left[1] = np.concatenate([ux + ex, zero]), np.concatenate([zero, ux + ex])
    left[2], left[3] = np.concatenate([ux * sx, zero]), np.concatenate([zero, ux * sx])
    left[6], left[7] = np.concatenate([ex, zero]), np.concatenate([zero, ex])
    right = np.zeros((8, HEIGHT))
    right[4], right[5] = uy + ey, uy * sy
    t["left"], t["right"] = left.astype(np.float32), right.astype(np.float32)
    split = np.concatenate([np.arange(0, DEPTH, 2), np.arange(1, DEPTH, 2)])
    t["cos"] = cosines[split][:, split].astype(np.float32)
    t["sy"] = sin_y.astype(np.float32)
    t["sx2"] = np.kron(np.eye(2), sin_x).astype(np.float32)
    return t


def halved(x):
    high = x.astype(BF16)
    return high, (x - high.astype(F32)).astype(BF16)


def dot(a, b, dims=((1,), (0,))):
    return lax.dot_general(a, b, (dims, ((), ())), preferred_element_type=F32)


def dot3(a, b, dims=((1,), (0,))):
    return dot(a[0], b[0], dims) + (dot(a[0], b[1], dims) + dot(a[1], b[0], dims))


def dot_exact(a, b, dims=((1,), (0,))):
    return lax.dot_general(
        a, b, (dims, ((), ())), precision=lax.Precision.HIGHEST, preferred_element_type=F32
    )


def lane_ids(shape):
    return lax.broadcasted_iota(jnp.int32, shape, len(shape) - 1)


def interior():
    row = lax.broadcasted_iota(jnp.int32, (WIDTH, HEIGHT), 0)
    return (row > 0) & (lane_ids((WIDTH, HEIGHT)) > 0)


def pair_lanes(parts):
    return jnp.concatenate(parts, 1)


def forward_kernel(vert, charge, surface, zh, zl, xh, xl, yh, yl, urh, url, uch, ucl, plane, base, msg, work):
    ztab, xtab, ytab = (zh[...], zl[...]), (xh[...], xl[...]), (yh[...], yl[...])
    for t in range(WIDTH // 16):
        sides = []
        for h in range(2):
            at = pl.ds(16 * t + 8 * h, 8)
            block = charge[:, at, :]
            block = jnp.concatenate(
                [block[:1] + surface[0:1, at, :], block[1:-1], block[-1:] + surface[1:2, at, :]], 0
            )
            sides.append(block.reshape(DEPTH * 8, HEIGHT))
        out = dot3(ztab, halved(pair_lanes(sides)))
        for h in range(2):
            side = out[:, HEIGHT * h:HEIGHT * (h + 1)]
            side = dot3(halved(side), ytab)
            work[:, 16 * t + 8 * h:16 * t + 8 * h + 8, :] = side.reshape(DEPTH, 8, HEIGHT)
    inner = interior()
    flat = plane[...]
    lane = lane_ids((8, HEIGHT))
    for t in range(DEPTH // 8):
        sides = [work[8 * t + 4 * h:8 * t + 4 * h + 4].reshape(4 * WIDTH, HEIGHT) for h in range(2)]
        out = dot3(xtab, halved(pair_lanes(sides)))
        for h in range(2):
            side = out[:, HEIGHT * h:HEIGHT * (h + 1)].reshape(4, WIDTH, HEIGHT)
            full = []
            corner = []
            for s in range(4):
                k = 8 * t + 4 * h + s
                one = jnp.where(inner, side[s] / (flat + vert[k]), side[s])
                base[k] = jnp.where(inner, one, 0.0)
                full.append(one)
                corner.append(one[0:1])
            full = jnp.concatenate(full, 0)
            parts = halved(full)
            rows = dot3((urh[...], url[...]), parts)
            own = jnp.concatenate(corner + [jnp.zeros((4, HEIGHT), F32)], 0)
            rows = jnp.where(lane == 0, own, rows)
            cols = dot3((uch[...], ucl[...]), parts, ((1,), (1,)))
            first = lane_ids((1, 4 * WIDTH)) % WIDTH == 0
            near = jnp.where(first, cols[2:3], cols[0:1])
            far = jnp.where(first, 0.0, cols[1:2])
            for g in range(2):
                at = slice(HEIGHT * g, HEIGHT * (g + 1))
                msg[4 * t + 2 * h + g] = jnp.concatenate(
                    [rows[2 * g:2 * g + 2], rows[4 + 2 * g:6 + 2 * g], near[:, at], far[:, at], jnp.zeros((2, HEIGHT), F32)],
                    0,
                )


def shift_x(n_gx, n_gy, field, by):
    cut = (by % n_gx) * n_gy
    return jnp.concatenate([field[cut:], field[:cut]], 0)


def shift_y(n_gx, n_gy, field, by):
    place = lax.broadcasted_iota(jnp.int32, field.shape, 0) % n_gy
    count = n_gx * n_gy
    ahead = by % count
    plain = jnp.concatenate([field[ahead:], field[:ahead]], 0)
    wrap = (by - n_gy if by > 0 else by + n_gy) % count
    wrapped = jnp.concatenate([field[wrap:], field[:wrap]], 0)
    edge = n_gy - 1 if by > 0 else 0
    return jnp.where(place == edge, wrapped, plain)


def turn_half(x):
    return jnp.concatenate([x[:, WIDTH:], x[:, :WIDTH]], 1)


def schur_modes(n_gx, n_gy, coef, table, row, col):
    row_coef, row_far, col_coef, col_far, row_sign, col_sign = coef
    sx = functools.partial(shift_x, n_gx, n_gy)
    sy = functools.partial(shift_y, n_gx, n_gy)
    count = n_gx * n_gy
    across = dot_exact(jnp.concatenate([col, col * col_sign], 0), table)
    along = dot_exact(jnp.concatenate([row, row * row_sign], 0), table, ((1,), (1,)))
    v = across[:count] + sx(across[count:], -1)
    w = along[:count] + sy(along[count:], -1)
    row_out = row_coef * row - row_far * (sx(row, 1) + sx(row, -1)) - v - row_sign * sy(v, 1)
    col_out = col_coef * col - col_far * (sy(col, 1) + sy(col, -1)) - w - col_sign * sx(w, 1)
    lane = lane_ids((count, HEIGHT))
    row_out = row_out - jnp.concatenate(
        [jnp.where(lane == 0, w, 0.0), jnp.where(lane == 0, turn_half(w), 0.0)], 1
    )
    col_out = jnp.where(
        lane == 0, row_out[:, :HEIGHT], jnp.where(lane == WIDTH, turn_half(row_out[:, HEIGHT:]), col_out)
    )
    return row_out, col_out


def owner_tables(own, pair, signs):
    inner = interior()
    parts = []
    for s in range(2):
        one = jnp.where(inner, pair[0] / (pair[2] + own[6 + s:7 + s]), pair[1])
        parts.append(one)
    blank = jnp.zeros((WIDTH, HEIGHT), F32)
    table = jnp.concatenate([pair_lanes([parts[0], blank]), pair_lanes([blank, parts[1]])], 0)
    coef = (
        pair_lanes([own[0:1], own[1:2]]),
        pair_lanes([own[2:3], own[3:4]]),
        own[4:5],
        own[5:6],
        pair_lanes([signs[0:1], signs[0:1]]),
        signs[1:2],
    )
    return coef, table


def start_modes(n_gx, n_gy, fields):
    sx = functools.partial(shift_x, n_gx, n_gy)
    sy = functools.partial(shift_y, n_gx, n_gy)
    row = pair_lanes([fields[0], fields[1]]) + sx(pair_lanes([fields[2], fields[3]]), -1)
    col = fields[4] + sy(fields[5], -1)
    return row, col


def inner_product(first, second):
    lane = lane_ids(first[1].shape)
    cols = jnp.where(lane % WIDTH == 0, 0.0, first[1] * second[1])
    rows = first[0] * second[0]
    return jnp.sum(rows[:, :HEIGHT] + rows[:, HEIGHT:] + cols)


def face_fields(n_gx, n_gy, pair):
    row, col = pair
    beyond = shift_x(n_gx, n_gy, row, 1)
    return [
        row[:, :HEIGHT], row[:, HEIGHT:], beyond[:, :HEIGHT], beyond[:, HEIGHT:],
        col, shift_y(n_gx, n_gy, col, 1),
    ]


def steps(sums):
    rr, rw, ww, wv = sums
    alpha = rr / rw
    after = alpha * alpha * ww - rr
    beta = after / rr
    curve = (1 + beta) * (1 + beta) * rw - 2 * (1 + beta) * alpha * ww + alpha * alpha * wv
    second = after / curve
    return alpha + second * (1 + beta), -second * alpha


def exchange_kernel(n_gx, n_gy, msg, own_ref, pair_ref, signs_ref, faces, rest, got, back, landed, sems):
    count = n_gx * n_gy
    gx, gy = lax.axis_index("gx"), lax.axis_index("gy")
    me = gx * n_gy + gy

    def partner(off):
        to = lax.rem(me + off, count)
        return to, {"gx": lax.div(to, n_gy), "gy": lax.rem(to, n_gy)}

    barrier = pltpu.get_barrier_semaphore()
    for off in range(1, count):
        pl.semaphore_signal(barrier, inc=1, device_id=partner(off)[1], device_id_type=pl.DeviceIdType.MESH)
    coef, table = owner_tables(own_ref[me], pair_ref[...], signs_ref[...])
    pl.semaphore_wait(barrier, count - 1)

    def spread(source, target, which):
        copies = []
        for off in range(1, count):
            to, device = partner(off)
            copies.append(
                pltpu.make_async_remote_copy(
                    src_ref=source.at[to],
                    dst_ref=target.at[me],
                    send_sem=sems.at[which, 0, off],
                    recv_sem=sems.at[which, 1, off],
                    device_id=device,
                    device_id_type=pl.DeviceIdType.MESH,
                )
            )
            copies[-1].start()
        target[me] = source[me]
        return copies

    first = spread(msg, got, 0)
    for copy in first:
        copy.wait_recv()
    fields = [got[:, f, :] for f in range(6)]
    r = start_modes(n_gx, n_gy, fields)
    w = schur_modes(n_gx, n_gy, coef, table, *r)
    v = schur_modes(n_gx, n_gy, coef, table, *w)
    for f, field in enumerate(face_fields(n_gx, n_gy, r)):
        back[:, f, :] = field
    for f, field in enumerate(face_fields(n_gx, n_gy, w)):
        back[:, 8 + f, :] = field
    back[:, 6, :] = v[0][:, :HEIGHT]
    back[:, 7, :] = v[0][:, HEIGHT:]
    back[:, 14, :] = v[1]
    sums = (inner_product(r, r), inner_product(r, w), inner_product(w, w), inner_product(w, v))
    lane = lane_ids((count, HEIGHT))
    back[:, 15, :] = sum(jnp.where(lane == s, value, 0.0) for s, value in enumerate(sums))
    second = spread(back, landed, 1)
    for copy in second:
        copy.wait_recv()
    for copy in first + second:
        copy.wait_send()
    faces[...], rest[...] = combine(landed[...])


def combine(landed):
    near, far = landed[:, :8], landed[:, 8:]
    total = jnp.sum(far[:, 7:8, :], 0)
    lane = lane_ids((1, HEIGHT))
    c0, c1 = steps([jnp.sum(jnp.where(lane == s, total, 0.0)) for s in range(4)])
    faces = c0 * near + c1 * far
    lead = near - c0 * far
    rest = jnp.concatenate(
        [lead[:, 0:2] - c1 * near[:, 6:8], lead[:, 4:5] - c1 * far[:, 6:7], jnp.zeros_like(near[:, :5])], 1
    )
    return faces, rest


def stacked(left, right):
    lh, ll = halved(left)
    rh, rl = halved(right)
    lhs = jnp.concatenate([lh.astype(F32), lh.astype(F32), ll.astype(F32)], 0).astype(BF16)
    rhs = jnp.concatenate([rh.astype(F32), rl.astype(F32), rh.astype(F32)], 0).astype(BF16)
    return dot(lhs, rhs, ((0,), (0,)))


def inverse_kernel(vert, base, faces, rest, left, right, zh, zl, xh, xl, yh, yl, plane, cos, sin_y, sin_x2, potential, residual, work):
    ztab, xtab, ytab = (zh[...], zl[...]), (xh[...], xl[...]), (yh[...], yl[...])
    inner = interior()
    flat = plane[...]
    lane = lane_ids((8, HEIGHT))
    sub = lax.broadcasted_iota(jnp.int32, (8, HEIGHT), 0)
    const_left, const_right = left[...], right[...]
    for t in range(DEPTH // 8):
        sides = []
        for h in range(2):
            blocks = []
            for g in range(2):
                o = 4 * t + 2 * h + g
                one = faces[o]
                lhs = jnp.where((sub >= 4) & (sub < 6) & (lane % WIDTH > 0), one, const_left)
                up = jnp.concatenate([one[2:], one[:2]], 0)
                rhs = jnp.where((sub < 4) & (lane > 0), one, const_right)
                rhs = jnp.where((sub >= 6) & (lane == 0), up, rhs)
                out = stacked(lhs, rhs)
                for s in range(2):
                    k = 2 * o + s
                    part = out[WIDTH * s:WIDTH * (s + 1)]
                    part = jnp.where(inner, part / (flat + vert[k]), part)
                    blocks.append(part + base[k])
            sides.append(jnp.concatenate(blocks, 0))
        out = dot3(xtab, halved(pair_lanes(sides)))
        for h in range(2):
            side = dot3(halved(out[:, HEIGHT * h:HEIGHT * (h + 1)]), ytab)
            work[8 * t + 4 * h:8 * t + 4 * h + 4] = side.reshape(4, WIDTH, HEIGHT)
    for t in range(WIDTH // 16):
        sides = [work[:, 16 * t + 8 * h:16 * t + 8 * h + 8, :].reshape(DEPTH * 8, HEIGHT) for h in range(2)]
        out = dot3(ztab, halved(pair_lanes(sides)))
        for h in range(2):
            side = out[:, HEIGHT * h:HEIGHT * (h + 1)]
            potential[:, 16 * t + 8 * h:16 * t + 8 * h + 8, :] = side.reshape(DEPTH, 8, HEIGHT)
    half = DEPTH // 2
    rows = jnp.concatenate([rest[:, 0, :], rest[:, 1, :]], 0)
    rows = dot_exact(cos[...], dot_exact(rows, sin_y[...]))
    cols = dot_exact(rest[:, 2, :], sin_x2[...])
    cols = dot_exact(cos[...], jnp.concatenate([cols[:, :WIDTH], cols[:, WIDTH:]], 0))
    cols = jnp.concatenate([cols[:half], cols[half:]], 1)
    cols = jnp.where(lane_ids((half, HEIGHT)) % WIDTH == 0, 0.0, cols)
    unit = jnp.where(lane == 0, 1.0, 0.0)
    mark = jnp.where(((sub == 0) & (lane == 0)) | ((sub == 1) & (lane == WIDTH)), 1.0, 0.0)
    for o in range(half):
        lhs = jnp.where(sub == 2, cols[o:o + 1], mark)
        rhs = jnp.where(sub == 0, rows[o:o + 1], jnp.where(sub == 1, rows[half + o:half + o + 1], jnp.where(sub == 2, unit, 0.0)))
        out = stacked(lhs, rhs)
        residual[2 * o] = out[:WIDTH]
        residual[2 * o + 1] = out[WIDTH:]


def on_device_modes(n_gx, n_gy, charge, surface_charge):
    t = host_tables()
    count = n_gx * n_gy
    block = jax.ShapeDtypeStruct(charge.shape, F32)
    small = jax.ShapeDtypeStruct((count, 8, HEIGHT), F32)
    params = dict(vmem_limit_bytes=48 * 1024 * 1024)
    base, msg = pl.pallas_call(
        functools.partial(forward_kernel, t["vert"]),
        out_shape=(block, small),
        scratch_shapes=[pltpu.VMEM(charge.shape, F32)],
        compiler_params=pltpu.CompilerParams(**params),
        name="forward",
    )(charge, surface_charge, *t["zf"], *t["x"], *t["y"], *t["ur"], *t["uc"], t["plane"])
    pair = np.concatenate([t["pair"], t["plane"][None]], 0)
    faces, rest = pl.pallas_call(
        functools.partial(exchange_kernel, n_gx, n_gy),
        out_shape=(small, small),
        scratch_shapes=[
            pltpu.VMEM((count, 8, HEIGHT), F32),
            pltpu.VMEM((count, 16, HEIGHT), F32),
            pltpu.VMEM((count, 16, HEIGHT), F32),
            pltpu.SemaphoreType.DMA((2, 2, count)),
        ],
        in_specs=[pl.BlockSpec(memory_space=pltpu.VMEM)] * 4,
        compiler_params=pltpu.CompilerParams(collective_id=0, has_side_effects=True, **params),
        name="exchange",
    )(msg, t["own"], pair, t["signs"])
    return pl.pallas_call(
        functools.partial(inverse_kernel, t["vert"]),
        out_shape=(block, block),
        scratch_shapes=[pltpu.VMEM(charge.shape, F32)],
        compiler_params=pltpu.CompilerParams(**params),
        name="inverse",
    )(base, faces, rest, t["left"], t["right"], *t["zi"], *t["x"], *t["y"], t["plane"], t["cos"], t["sy"], t["sx2"])


def solution(mesh):
    count = mesh.shape["gx"] * mesh.shape["gy"]
    per_device = functools.partial(on_device_modes, mesh.shape["gx"], mesh.shape["gy"])
    if 2 * count != DEPTH:
        per_device = on_device
    in_specs = (P(None, ("slab", "gx"), "gy"), P(None, ("slab", "gx"), "gy"))
    out_specs = (P(None, ("slab", "gx"), "gy"), P(None, ("slab", "gx"), "gy"))
    return jax.shard_map(
        per_device, mesh=mesh, in_specs=in_specs, out_specs=out_specs, check_vma=False
    )
```

profile of v0, /device:TPU:0, one launch (start us, length us, event | category | flops | bytes accessed | tf_op | source)
XLA Modules:
  0.0 36.4 jit_solution(16865331676173826255)
XLA Ops:
  0.6 0.0 copy-start.5
  0.6 0.0 copy-start.23
  0.7 0.7 %copy-done.5 = f32[64,128]{1,0:T(8,128)S(1)} copy-done((f32[64,128]{1,0:T(8,128)S(1)}, f32[64,128]{1,0:T(8,128)}, u32[]{:S(2)}) %copy-start.5) | copy-done | bytes 32792
  1.4 0.0 copy-done.23
  1.4 0.0 copy-start
  1.4 1.2 %copy-done = f32[32,64,128]{2,1,0:T(8,128)S(1)} copy-done((f32[32,64,128]{2,1,0:T(8,128)S(1)}, f32[32,64,128]{2,1,0:T(8,128)}, u32[]{:S(2)}) %copy-start) | copy-done | bytes 1048600
  2.6 0.0 copy-start.1
  2.6 0.9 %copy-done.1 = bf16[256,256]{1,0:T(8,128)(2,1)S(1)} copy-done((bf16[256,256]{1,0:T(8,128)(2,1)S(1)}, bf16[256,256]{1,0:T(8,128)(2,1)}, u32[]{:S(2)}) %copy-start.1) | copy-done | bytes 131096
  3.5 0.0 copy-start.3
  3.5 0.9 %copy-done.3 = bf16[256,256]{1,0:T(8,128)(2,1)S(1)} copy-done((bf16[256,256]{1,0:T(8,128)(2,1)S(1)}, bf16[256,256]{1,0:T(8,128)(2,1)}, u32[]{:S(2)}) %copy-start.3) | copy-done | bytes 131096
  4.4 0.0 copy-start.6
  4.4 0.8 %copy-done.6 = bf16[128,128]{1,0:T(8,128)(2,1)S(1)} copy-done((bf16[128,128]{1,0:T(8,128)(2,1)S(1)}, bf16[128,128]{1,0:T(8,128)(2,1)}, u32[]{:S(2)}) %copy-start.6) | copy-done | bytes 32792
  5.2 0.0 copy-start.8
  5.2 0.8 %copy-done.8 = bf16[128,128]{1,0:T(8,128)(2,1)S(1)} copy-done((bf16[128,128]{1,0:T(8,128)(2,1)S(1)}, bf16[128,128]{1,0:T(8,128)(2,1)}, u32[]{:S(2)}) %copy-start.8) | copy-done | bytes 32792
  5.9 0.0 copy-start.10
  5.9 0.9 %copy-done.10 = bf16[256,256]{1,0:T(8,128)(2,1)S(1)} copy-done((bf16[256,256]{1,0:T(8,128)(2,1)S(1)}, bf16[256,256]{1,0:T(8,128)(2,1)}, u32[]{:S(2)}) %copy-start.10) | copy-done | bytes 131096
  6.9 0.0 copy-start.11
  6.9 0.9 %copy-done.11 = bf16[256,256]{1,0:T(8,128)(2,1)S(1)} copy-done((bf16[256,256]{1,0:T(8,128)(2,1)S(1)}, bf16[256,256]{1,0:T(8,128)(2,1)}, u32[]{:S(2)}) %copy-start.11) | copy-done | bytes 131096
  7.8 0.0 copy-start.18
  7.8 0.8 %copy-done.18 = f32[2,64,128]{2,1,0:T(8,128)S(1)} copy-done((f32[2,64,128]{2,1,0:T(8,128)S(1)}, f32[2,64,128]{2,1,0:T(8,128)}, u32[]{:S(2)}) %copy-start.18) | copy-done | bytes 65560
  8.6 0.0 copy-start.24
  8.6 0.7 %copy-done.24 = bf16[16,128]{1,0:T(8,128)(2,1)S(1)} copy-done((bf16[16,128]{1,0:T(8,128)(2,1)S(1)}, bf16[16,128]{1,0:T(8,128)(2,1)}, u32[]{:S(2)}) %copy-start.24) | copy-done | bytes 4120
  9.3 0.0 copy-start.25
  9.3 0.7 %copy-done.25 = bf16[8,256]{1,0:T(8,128)(2,1)S(1)} copy-done((bf16[8,256]{1,0:T(8,128)(2,1)S(1)}, bf16[8,256]{1,0:T(8,128)(2,1)}, u32[]{:S(2)}) %copy-start.25) | copy-done | bytes 4120
  10.0 0.0 copy-start.26
  10.0 0.7 %copy-done.26 = bf16[8,256]{1,0:T(8,128)(2,1)S(1)} copy-done((bf16[8,256]{1,0:T(8,128)(2,1)S(1)}, bf16[8,256]{1,0:T(8,128)(2,1)}, u32[]{:S(2)}) %copy-start.26) | copy-done | bytes 4120
  10.7 0.0 copy-start.14
  10.7 0.0 copy-start.17
  10.7 0.0 copy-start.22
  10.7 0.0 copy-start.4
  10.7 0.0 copy-start.12
  10.7 0.0 copy-start.13
  10.7 0.0 copy-start.15
  10.7 0.0 copy-start.16
  10.7 3.5 %forward.1 = (f32[32,64,128]{2,1,0:T(8,128)S(1)}, f32[16,8,128]{2,1,0:T(8,128)S(1)}) custom-call(f32[32,64,128]{2,1,0:T(8,128)S(1)} %copy-done, f32[2,64,128]{2,1,0:T(8,128)S(1)} %copy-done.18, bf16[256,256]{1,0:T(8,128)(2,1)S(1)} %copy-done.11, bf16[256,256]{1,0:T(8,128)(2,1)S(1)} %copy-done.10, bf16[256,256]{1,0:T(8,128)(2,1)S(1)} %copy-done.3, ...), custom_call_target="tpu_custom_call" | custom-call | tf_op jit(solution)/shard_map/forward/pallas_call | solution.py:521
  14.3 0.0 copy-start.2
  14.3 0.0 copy-done.14
  14.3 0.0 copy-done.17
  14.3 0.0 copy-done.22
  14.3 0.0 copy-start.7
  14.3 0.0 copy-start.9
  14.3 0.0 copy-start.19
  14.3 0.0 copy-start.20
  14.3 0.0 copy-start.21
  14.4 16.5 %exchange.1 = (f32[16,8,128]{2,1,0:T(8,128)S(1)}, f32[16,8,128]{2,1,0:T(8,128)S(1)}) custom-call(f32[16,8,128]{2,1,0:T(8,128)S(1)} %get-tuple-element.7.msg, f32[16,8,128]{2,1,0:T(8,128)S(1)} %copy-done.17, f32[3,64,128]{2,1,0:T(8,128)S(1)} %copy-done.14, f32[8,128]{1,0:T(8,128)S(1)} %copy-done.22), custom_call_target="tpu_custom_call" | custom-call | tf_op jit(solution)/shard_map/exchange/pallas_call | solution.py:529
  30.9 0.0 copy-done.4
  30.9 0.0 copy-done.12
  30.9 0.0 copy-done.13
  30.9 0.0 copy-done.15
  30.9 0.0 copy-done.16
  30.9 0.0 copy-done.2
  30.9 0.0 copy-done.7
  30.9 0.0 copy-done.9
  30.9 0.0 copy-done.19
  31.0 0.0 copy-done.20
  31.0 0.0 copy-done.21
  31.0 5.4 %inverse.1 = (f32[32,64,128]{2,1,0:T(8,128)}, f32[32,64,128]{2,1,0:T(8,128)}) custom-call(f32[32,64,128]{2,1,0:T(8,128)S(1)} %get-tuple-element.6.base, f32[16,8,128]{2,1,0:T(8,128)S(1)} %get-tuple-element.8.faces, f32[16,8,128]{2,1,0:T(8,128)S(1)} %get-tuple-element.9.rest, f32[8,128]{1,0:T(8,128)S(1)} %copy-done.21, f32[8,128]{1,0:T(8,128)S(1)} %copy-done.20, ...), custom_call_target="tpu_custom_call" | custom-call | tf_op jit(solution)/shard_map/inverse/pallas_call | solution.py:542
Async XLA Ops:
  0.6 0.8 %copy-start.5 = (f32[64,128]{1,0:T(8,128)S(1)}, f32[64,128]{1,0:T(8,128)}, u32[]{:S(2)}) copy-start(f32[64,128]{1,0:T(8,128)} %constant.52.clone.plane) | copy-start | bytes 98308
  0.6 0.8 %copy-start.23 = (bf16[16,128]{1,0:T(8,128)(2,1)S(1)}, bf16[16,128]{1,0:T(8,128)(2,1)}, u32[]{:S(2)}) copy-start(bf16[16,128]{1,0:T(8,128)(2,1)} %constant.51.clone.ucl) | copy-start | bytes 12292
  1.4 1.2 %copy-start = (f32[32,64,128]{2,1,0:T(8,128)S(1)}, f32[32,64,128]{2,1,0:T(8,128)}, u32[]{:S(2)}) copy-start(f32[32,64,128]{2,1,0:T(8,128)} %charge.1) | copy-start | bytes 3145732
  2.6 0.9 %copy-start.1 = (bf16[256,256]{1,0:T(8,128)(2,1)S(1)}, bf16[256,256]{1,0:T(8,128)(2,1)}, u32[]{:S(2)}) copy-start(bf16[256,256]{1,0:T(8,128)(2,1)} %constant.45.clone.xl) | copy-start | bytes 393220
  3.5 0.9 %copy-start.3 = (bf16[256,256]{1,0:T(8,128)(2,1)S(1)}, bf16[256,256]{1,0:T(8,128)(2,1)}, u32[]{:S(2)}) copy-start(bf16[256,256]{1,0:T(8,128)(2,1)} %constant.44.clone.xh) | copy-start | bytes 393220
  4.4 0.8 %copy-start.6 = (bf16[128,128]{1,0:T(8,128)(2,1)S(1)}, bf16[128,128]{1,0:T(8,128)(2,1)}, u32[]{:S(2)}) copy-start(bf16[128,128]{1,0:T(8,128)(2,1)} %constant.47.clone.yl) | copy-start | bytes 98308
  5.2 0.8 %copy-start.8 = (bf16[128,128]{1,0:T(8,128)(2,1)S(1)}, bf16[128,128]{1,0:T(8,128)(2,1)}, u32[]{:S(2)}) copy-start(bf16[128,128]{1,0:T(8,128)(2,1)} %constant.46.clone.yh) | copy-start | bytes 98308
  5.9 0.9 %copy-start.10 = (bf16[256,256]{1,0:T(8,128)(2,1)S(1)}, bf16[256,256]{1,0:T(8,128)(2,1)}, u32[]{:S(2)}) copy-start(bf16[256,256]{1,0:T(8,128)(2,1)} %constant.43.clone.zl) | copy-start | bytes 393220
  6.9 0.9 %copy-start.11 = (bf16[256,256]{1,0:T(8,128)(2,1)S(1)}, bf16[256,256]{1,0:T(8,128)(2,1)}, u32[]{:S(2)}) copy-start(bf16[256,256]{1,0:T(8,128)(2,1)} %constant.42.clone.zh) | copy-start | bytes 393220
  7.8 0.8 %copy-start.18 = (f32[2,64,128]{2,1,0:T(8,128)S(1)}, f32[2,64,128]{2,1,0:T(8,128)}, u32[]{:S(2)}) copy-start(f32[2,64,128]{2,1,0:T(8,128)} %surface.1) | copy-start | bytes 196612
  8.6 0.7 %copy-start.24 = (bf16[16,128]{1,0:T(8,128)(2,1)S(1)}, bf16[16,128]{1,0:T(8,128)(2,1)}, u32[]{:S(2)}) copy-start(bf16[16,128]{1,0:T(8,128)(2,1)} %constant.50.clone.uch) | copy-start | bytes 12292
  9.3 0.7 %copy-start.25 = (bf16[8,256]{1,0:T(8,128)(2,1)S(1)}, bf16[8,256]{1,0:T(8,128)(2,1)}, u32[]{:S(2)}) copy-start(bf16[8,256]{1,0:T(8,128)(2,1)} %constant.49.clone.url) | copy-start | bytes 12292
  10.0 0.7 %copy-start.26 = (bf16[8,256]{1,0:T(8,128)(2,1)S(1)}, bf16[8,256]{1,0:T(8,128)(2,1)}, u32[]{:S(2)}) copy-start(bf16[8,256]{1,0:T(8,128)(2,1)} %constant.48.clone.urh) | copy-start | bytes 12292
  10.7 3.6 %copy-start.14 = (f32[3,64,128]{2,1,0:T(8,128)S(1)}, f32[3,64,128]{2,1,0:T(8,128)}, u32[]{:S(2)}) copy-start(f32[3,64,128]{2,1,0:T(8,128)} %constant.54.clone.pair_ref) | copy-start | bytes 294916
  10.7 3.6 %copy-start.17 = (f32[16,8,128]{2,1,0:T(8,128)S(1)}, f32[16,8,128]{2,1,0:T(8,128)}, u32[]{:S(2)}) copy-start(f32[16,8,128]{2,1,0:T(8,128)} %constant.53.clone.own_ref) | copy-start | bytes 196612
  10.7 3.6 %copy-start.22 = (f32[8,128]{1,0:T(8,128)S(1)}, f32[8,128]{1,0:T(8,128)}, u32[]{:S(2)}) copy-start(f32[8,128]{1,0:T(8,128)} %constant.55.clone.signs_ref) | copy-start | bytes 12292
  10.7 20.2 %copy-start.4 = (bf16[256,256]{1,0:T(8,128)(2,1)S(1)}, bf16[256,256]{1,0:T(8,128)(2,1)}, u32[]{:S(2)}) copy-start(bf16[256,256]{1,0:T(8,128)(2,1)} %constant.44.clone.xh) | copy-start | bytes 393220
  10.7 20.2 %copy-start.12 = (bf16[256,256]{1,0:T(8,128)(2,1)S(1)}, bf16[256,256]{1,0:T(8,128)(2,1)}, u32[]{:S(2)}) copy-start(bf16[256,256]{1,0:T(8,128)(2,1)} %constant.59.clone.zl) | copy-start | bytes 393220
  10.7 20.2 %copy-start.13 = (bf16[256,256]{1,0:T(8,128)(2,1)S(1)}, bf16[256,256]{1,0:T(8,128)(2,1)}, u32[]{:S(2)}) copy-start(bf16[256,256]{1,0:T(8,128)(2,1)} %constant.58.clone.zh) | copy-start | bytes 393220
  10.7 20.2 %copy-start.15 = (f32[128,128]{1,0:T(8,128)S(1)}, f32[128,128]{1,0:T(8,128)}, u32[]{:S(2)}) copy-start(f32[128,128]{1,0:T(8,128)} %constant.62.clone.sin_x2) | copy-start | bytes 196612
  10.7 20.2 %copy-start.16 = (f32[128,128]{1,0:T(8,128)S(1)}, f32[128,128]{1,0:T(8,128)}, u32[]{:S(2)}) copy-start(f32[128,128]{1,0:T(8,128)} %constant.61.clone.sin_y) | copy-start | bytes 196612
  14.3 16.7 %copy-start.2 = (bf16[256,256]{1,0:T(8,128)(2,1)S(1)}, bf16[256,256]{1,0:T(8,128)(2,1)}, u32[]{:S(2)}) copy-start(bf16[256,256]{1,0:T(8,128)(2,1)} %constant.45.clone.xl) | copy-start | bytes 393220
  14.3 16.6 %copy-start.7 = (bf16[128,128]{1,0:T(8,128)(2,1)S(1)}, bf16[128,128]{1,0:T(8,128)(2,1)}, u32[]{:S(2)}) copy-start(bf16[128,128]{1,0:T(8,128)(2,1)} %constant.47.clone.yl) | copy-start | bytes 98308
  14.3 16.6 %copy-start.9 = (bf16[128,128]{1,0:T(8,128)(2,1)S(1)}, bf16[128,128]{1,0:T(8,128)(2,1)}, u32[]{:S(2)}) copy-start(bf16[128,128]{1,0:T(8,128)(2,1)} %constant.46.clone.yh) | copy-start | bytes 98308
  14.3 16.6 %copy-start.19 = (f32[32,32]{1,0:T(8,128)S(1)}, f32[32,32]{1,0:T(8,128)}, u32[]{:S(2)}) copy-start(f32[32,32]{1,0:T(8,128)} %constant.60.clone.cos) | copy-start | bytes 12292
  14.3 16.6 %copy-start.20 = (f32[8,128]{1,0:T(8,128)S(1)}, f32[8,128]{1,0:T(8,128)}, u32[]{:S(2)}) copy-start(f32[8,128]{1,0:T(8,128)} %constant.57.clone.right) | copy-start | bytes 12292
  14.3 16.6 %copy-start.21 = (f32[8,128]{1,0:T(8,128)S(1)}, f32[8,128]{1,0:T(8,128)}, u32[]{:S(2)}) copy-start(f32[8,128]{1,0:T(8,128)} %constant.56.clone.left) | copy-start | bytes 12292
where the time goes:
time: 37 us; the launch traced here: 36.4 us
  Pallas kernels  25.5 us (69%)
  local copies, waits for them, and re-layouts  10.1 us (27%)
  between operations  0.86 us (2%)
    pallas_call x1, Pallas kernels, on_device_modes(): pl.pallas_call(functools.partial(exchange_kernel, n_gx, n_gy), out_shape=...  16.5 us
    unnamed x54, local copies, waits for them, and re-layouts  10.1 us
    pallas_call x1, Pallas kernels, on_device_modes(): pl.pallas_call(functools.partial(inverse_kernel, t['vert']), out_shape=(b...  5.44 us
    pallas_call x1, Pallas kernels, on_device_modes(): pl.pallas_call(functools.partial(forward_kernel, t['vert']), out_shape=(b...  3.53 us

commit v1 on v0

--- a/solution.py
+++ b/solution.py
@@ -154,21 +154,22 @@
     sx[0] = sy[0] = 0.0
     ex, ey = np.eye(WIDTH)[0], np.eye(HEIGHT)[0]
     t = {}
-    t["zf"] = halves(np.kron(cosines.T, np.eye(8)))
-    t["zi"] = halves(np.kron(cosines, np.eye(8)))
-    t["x"] = halves(np.kron(np.eye(4), sin_x))
-    t["y"] = halves(sin_y)
+    t["zf"] = np.stack(halves(np.kron(cosines.T, np.eye(8))))
+    t["zi"] = np.stack(halves(np.kron(cosines, np.eye(8))))
+    t["x"] = np.stack(halves(np.kron(np.eye(4), sin_x)))
+    t["y"] = np.stack(halves(sin_y))
     plane = SCREEN + across[:, None] + along[None, :]
     t["plane"] = plane.astype(np.float32)
-    t["vert"] = [float(v) for v in vertical]
-    t["ur"] = halves(np.concatenate([np.kron(np.eye(4), (ux + ex)[None]), np.kron(np.eye(4), (ux * sx)[None])], 0))
+    ur = np.concatenate([np.kron(np.eye(4), (ux + ex)[None]), np.kron(np.eye(4), (ux * sx)[None]), np.zeros((8, 4 * WIDTH))], 0)
+    t["ur"] = np.stack(halves(ur))
     uc = np.zeros((16, HEIGHT))
     uc[0], uc[1], uc[2] = uy + ey, uy * sy, ey
-    t["uc"] = halves(uc)
+    t["uc"] = np.stack(halves(uc))
     spec = plane[None] + vertical[:, None, None]
     inner = np.zeros((WIDTH, HEIGHT))
     inner[1:, 1:] = 1.0
     inv = inner / spec
+    t["inv"] = np.where(inner > 0, inv, 1.0).astype(np.float32)
     row_near = np.einsum("a,kab->kb", ux * ux, inv)
     row_far = np.einsum("a,kab->kb", ux * ux * sx, inv)
     col_near = np.einsum("b,kab->ka", uy * uy, inv)
@@ -238,9 +239,22 @@
     return jnp.concatenate(parts, 1)
 
 
-def forward_kernel(vert, charge, surface, zh, zl, xh, xl, yh, yl, urh, url, uch, ucl, plane, base, msg, work):
-    ztab, xtab, ytab = (zh[...], zl[...]), (xh[...], xl[...]), (yh[...], yl[...])
+def forward_kernel(
+    charge_hbm, surface_hbm, z_hbm, x_hbm, y_hbm, ur_hbm, uc_hbm, inv_hbm, base, msg,
+    charge, surface, z, x, y, ur, uc, inv, work, sems,
+):
+    pairs = [(z_hbm, z), (surface_hbm, surface)]
+    pairs += [(charge_hbm.at[:, pl.ds(16 * t, 16), :], charge.at[:, pl.ds(16 * t, 16), :]) for t in range(WIDTH // 16)]
+    pairs += [(y_hbm, y), (x_hbm, x), (ur_hbm, ur), (uc_hbm, uc)]
+    pairs += [(inv_hbm.at[pl.ds(8 * t, 8)], inv.at[pl.ds(8 * t, 8)]) for t in range(DEPTH // 8)]
+    copies = [pltpu.make_async_copy(s, d, sems.at[n]) for n, (s, d) in enumerate(pairs)]
+    for copy in copies:
+        copy.start()
+    copies[0].wait()
+    copies[1].wait()
+    ztab = (z[0], z[1])
     for t in range(WIDTH // 16):
+        copies[2 + t].wait()
         sides = []
         for h in range(2):
             at = pl.ds(16 * t + 8 * h, 8)
@@ -250,14 +264,20 @@
             )
             sides.append(block.reshape(DEPTH * 8, HEIGHT))
         out = dot3(ztab, halved(pair_lanes(sides)))
+        if t == 0:
+            copies[6].wait()
+            ytab = (y[0], y[1])
         for h in range(2):
             side = out[:, HEIGHT * h:HEIGHT * (h + 1)]
             side = dot3(halved(side), ytab)
             work[:, 16 * t + 8 * h:16 * t + 8 * h + 8, :] = side.reshape(DEPTH, 8, HEIGHT)
+    for copy in copies[7:10]:
+        copy.wait()
+    xtab, utab, ctab = (x[0], x[1]), (ur[0], ur[1]), (uc[0], uc[1])
     inner = interior()
-    flat = plane[...]
     lane = lane_ids((8, HEIGHT))
     for t in range(DEPTH // 8):
+        copies[10 + t].wait()
         sides = [work[8 * t + 4 * h:8 * t + 4 * h + 4].reshape(4 * WIDTH, HEIGHT) for h in range(2)]
         out = dot3(xtab, halved(pair_lanes(sides)))
         for h in range(2):
@@ -266,16 +286,16 @@
             corner = []
             for s in range(4):
                 k = 8 * t + 4 * h + s
-                one = jnp.where(inner, side[s] / (flat + vert[k]), side[s])
+                one = side[s] * inv[k]
                 base[k] = jnp.where(inner, one, 0.0)
                 full.append(one)
                 corner.append(one[0:1])
             full = jnp.concatenate(full, 0)
             parts = halved(full)
-            rows = dot3((urh[...], url[...]), parts)
+            rows = dot3(utab, parts)
             own = jnp.concatenate(corner + [jnp.zeros((4, HEIGHT), F32)], 0)
-            rows = jnp.where(lane == 0, own, rows)
-            cols = dot3((uch[...], ucl[...]), parts, ((1,), (1,)))
+            rows = jnp.where(lane == 0, own, rows[:8])
+            cols = dot3(ctab, parts, ((1,), (1,)))
             first = lane_ids((1, 4 * WIDTH)) % WIDTH == 0
             near = jnp.where(first, cols[2:3], cols[0:1])
             far = jnp.where(first, 0.0, cols[1:2])
@@ -381,7 +401,7 @@
     return alpha + second * (1 + beta), -second * alpha
 
 
-def exchange_kernel(n_gx, n_gy, msg, own_ref, pair_ref, signs_ref, faces, rest, got, back, landed, sems):
+def exchange_kernel(n_gx, n_gy, msg, own_ref, pair_ref, signs_ref, faces, rest, got, back_r, back_w, back_v, landed_r, landed_w, landed_v, sems):
     count = n_gx * n_gy
     gx, gy = lax.axis_index("gx"), lax.axis_index("gy")
     me = gx * n_gy + gy
@@ -419,37 +439,40 @@
         copy.wait_recv()
     fields = [got[:, f, :] for f in range(6)]
     r = start_modes(n_gx, n_gy, fields)
+    for f, field in enumerate(face_fields(n_gx, n_gy, r)):
+        back_r[:, f, :] = field
+    second = spread(back_r, landed_r, 1)
     w = schur_modes(n_gx, n_gy, coef, table, *r)
+    for f, field in enumerate(face_fields(n_gx, n_gy, w)):
+        back_w[:, f, :] = field
+    second += spread(back_w, landed_w, 2)
     v = schur_modes(n_gx, n_gy, coef, table, *w)
-    for f, field in enumerate(face_fields(n_gx, n_gy, r)):
-        back[:, f, :] = field
-    for f, field in enumerate(face_fields(n_gx, n_gy, w)):
-        back[:, 8 + f, :] = field
-    back[:, 6, :] = v[0][:, :HEIGHT]
-    back[:, 7, :] = v[0][:, HEIGHT:]
-    back[:, 14, :] = v[1]
+    back_v[:, 0, :] = v[0][:, :HEIGHT]
+    back_v[:, 1, :] = v[0][:, HEIGHT:]
+    back_v[:, 2, :] = v[1]
     sums = (inner_product(r, r), inner_product(r, w), inner_product(w, w), inner_product(w, v))
     lane = lane_ids((count, HEIGHT))
-    back[:, 15, :] = sum(jnp.where(lane == s, value, 0.0) for s, value in enumerate(sums))
-    second = spread(back, landed, 1)
+    back_v[:, 3, :] = sum(jnp.where(lane == s, value, 0.0) for s, value in enumerate(sums))
+    second += spread(back_v, landed_v, 3)
     for copy in second:
         copy.wait_recv()
     for copy in first + second:
         copy.wait_send()
-    faces[...], rest[...] = combine(landed[...])
-
-
-def combine(landed):
-    near, far = landed[:, :8], landed[:, 8:]
-    total = jnp.sum(far[:, 7:8, :], 0)
+    faces[...], rest[...] = combine(landed_r[...], landed_w[...], landed_v[...])
+
+
+def combine(r, w, v):
+    total = jnp.sum(v[:, 3:4, :], 0)
     lane = lane_ids((1, HEIGHT))
     c0, c1 = steps([jnp.sum(jnp.where(lane == s, total, 0.0)) for s in range(4)])
-    faces = c0 * near + c1 * far
-    lead = near - c0 * far
+    sub = lax.broadcasted_iota(jnp.int32, r.shape, 1)
+    r = jnp.where(sub < 6, r, 0.0)
+    w = jnp.where(sub < 6, w, 0.0)
+    lead = r - c0 * w
     rest = jnp.concatenate(
-        [lead[:, 0:2] - c1 * near[:, 6:8], lead[:, 4:5] - c1 * far[:, 6:7], jnp.zeros_like(near[:, :5])], 1
-    )
-    return faces, rest
+        [lead[:, 0:2] - c1 * v[:, 0:2], lead[:, 4:5] - c1 * v[:, 2:3], jnp.zeros_like(r[:, :5])], 1
+    )
+    return c0 * r + c1 * w, rest
 
 
 def stacked(left, right):
@@ -460,10 +483,8 @@
     return dot(lhs, rhs, ((0,), (0,)))
 
 
-def inverse_kernel(vert, base, faces, rest, left, right, zh, zl, xh, xl, yh, yl, plane, cos, sin_y, sin_x2, potential, residual, work):
-    ztab, xtab, ytab = (zh[...], zl[...]), (xh[...], xl[...]), (yh[...], yl[...])
-    inner = interior()
-    flat = plane[...]
+def inverse_kernel(base, faces, rest, left, right, z, x, y, inv, cos, sin_y, sin_x2, potential, residual, work):
+    ztab, xtab, ytab = (z[0], z[1]), (x[0], x[1]), (y[0], y[1])
     lane = lane_ids((8, HEIGHT))
     sub = lax.broadcasted_iota(jnp.int32, (8, HEIGHT), 0)
     const_left, const_right = left[...], right[...]
@@ -481,9 +502,7 @@
                 out = stacked(lhs, rhs)
                 for s in range(2):
                     k = 2 * o + s
-                    part = out[WIDTH * s:WIDTH * (s + 1)]
-                    part = jnp.where(inner, part / (flat + vert[k]), part)
-                    blocks.append(part + base[k])
+                    blocks.append(out[WIDTH * s:WIDTH * (s + 1)] * inv[k] + base[k])
             sides.append(jnp.concatenate(blocks, 0))
         out = dot3(xtab, halved(pair_lanes(sides)))
         for h in range(2):
@@ -518,34 +537,44 @@
     block = jax.ShapeDtypeStruct(charge.shape, F32)
     small = jax.ShapeDtypeStruct((count, 8, HEIGHT), F32)
     params = dict(vmem_limit_bytes=48 * 1024 * 1024)
+    hbm = pl.BlockSpec(memory_space=pltpu.HBM)
     base, msg = pl.pallas_call(
-        functools.partial(forward_kernel, t["vert"]),
+        forward_kernel,
         out_shape=(block, small),
-        scratch_shapes=[pltpu.VMEM(charge.shape, F32)],
+        in_specs=[hbm] * 8,
+        scratch_shapes=[
+            pltpu.VMEM(charge.shape, F32),
+            pltpu.VMEM(surface_charge.shape, F32),
+            pltpu.VMEM(t["zf"].shape, BF16),
+            pltpu.VMEM(t["x"].shape, BF16),
+            pltpu.VMEM(t["y"].shape, BF16),
+            pltpu.VMEM(t["ur"].shape, BF16),
+            pltpu.VMEM(t["uc"].shape, BF16),
+            pltpu.VMEM(charge.shape, F32),
+            pltpu.VMEM(charge.shape, F32),
+            pltpu.SemaphoreType.DMA((14,)),
+        ],
         compiler_params=pltpu.CompilerParams(**params),
         name="forward",
-    )(charge, surface_charge, *t["zf"], *t["x"], *t["y"], *t["ur"], *t["uc"], t["plane"])
+    )(charge, surface_charge, t["zf"], t["x"], t["y"], t["ur"], t["uc"], t["inv"])
     pair = np.concatenate([t["pair"], t["plane"][None]], 0)
+    eight, four = (count, 8, HEIGHT), (count, 4, HEIGHT)
     faces, rest = pl.pallas_call(
         functools.partial(exchange_kernel, n_gx, n_gy),
         out_shape=(small, small),
-        scratch_shapes=[
-            pltpu.VMEM((count, 8, HEIGHT), F32),
-            pltpu.VMEM((count, 16, HEIGHT), F32),
-            pltpu.VMEM((count, 16, HEIGHT), F32),
-            pltpu.SemaphoreType.DMA((2, 2, count)),
-        ],
+        scratch_shapes=[pltpu.VMEM(shape, F32) for shape in (eight, eight, eight, four, eight, eight, four)]
+        + [pltpu.SemaphoreType.DMA((4, 2, count))],
         in_specs=[pl.BlockSpec(memory_space=pltpu.VMEM)] * 4,
         compiler_params=pltpu.CompilerParams(collective_id=0, has_side_effects=True, **params),
         name="exchange",
     )(msg, t["own"], pair, t["signs"])
     return pl.pallas_call(
-        functools.partial(inverse_kernel, t["vert"]),
+        inverse_kernel,
         out_shape=(block, block),
         scratch_shapes=[pltpu.VMEM(charge.shape, F32)],
         compiler_params=pltpu.CompilerParams(**params),
         name="inverse",
-    )(base, faces, rest, t["left"], t["right"], *t["zi"], *t["x"], *t["y"], t["plane"], t["cos"], t["sy"], t["sx2"])
+    )(base, faces, rest, t["left"], t["right"], t["zi"], t["x"], t["y"], t["inv"], t["cos"], t["sy"], t["sx2"])
 
 
 def solution(mesh):

time: 37 us -> 37.8 us (1.022)
  Pallas kernels: 25.5 us -> 29.1 us
  local copies, waits for them, and re-layouts: 10.1 us -> 7.49 us
    unnamed x54 -> x36, local copies, waits for them, and re-layouts: 10.1 us -> 7.49 us
    pallas_call x2, Pallas kernels: 8.97 us -> 11.3 us  [the longest x1 5.86 us: on_device_modes(): pl.pallas_call(forward_kernel, out_shape=(block, small), in_specs=[hbm] *...]
    pallas_call x1, Pallas kernels: 16.5 us -> 17.8 us  [on_device_modes(): pl.pallas_call(functools.partial(exchange_kernel, n_gx, n_gy), out_shape=...]
where the time goes in v1:
time: 37.8 us; the launch traced here: 37.3 us
  Pallas kernels  29.1 us (77%)
  local copies, waits for them, and re-layouts  7.49 us (20%)
  between operations  0.79 us (2%)
    pallas_call x1, Pallas kernels, on_device_modes(): pl.pallas_call(functools.partial(exchange_kernel, n_gx, n_gy), out_shape=...  17.8 us
    unnamed x36, local copies, waits for them, and re-layouts  7.49 us
    pallas_call x1, Pallas kernels, on_device_modes(): pl.pallas_call(forward_kernel, out_shape=(block, small), in_specs=[hbm] *...  5.86 us
    pallas_call x1, Pallas kernels, on_device_modes(): pl.pallas_call(inverse_kernel, out_shape=(block, block), scratch_shapes=[...  5.42 us

profile of v1, /device:TPU:0, one launch (start us, length us, event | category | flops | bytes accessed | tf_op | source)
XLA Modules:
  0.0 37.3 jit_solution(18001416371022316430)
XLA Ops:
  0.6 0.0 copy-start.13
  0.6 0.7 %copy-done.13 = bf16[2,16,256]{2,1,0:T(8,128)(2,1)S(1)} copy-done((bf16[2,16,256]{2,1,0:T(8,128)(2,1)S(1)}, bf16[2,16,256]{2,1,0:T(8,128)(2,1)}, u32[]{:S(2)}) %copy-start.13) | copy-done | bytes 16408
  1.4 0.0 copy-start
  1.4 1.2 %copy-done = f32[32,64,128]{2,1,0:T(8,128)S(1)} copy-done((f32[32,64,128]{2,1,0:T(8,128)S(1)}, f32[32,64,128]{2,1,0:T(8,128)}, u32[]{:S(2)}) %copy-start) | copy-done | bytes 1048600
  2.6 0.0 copy-start.2
  2.6 1.2 %copy-done.2 = f32[32,64,128]{2,1,0:T(8,128)S(1)} copy-done((f32[32,64,128]{2,1,0:T(8,128)S(1)}, f32[32,64,128]{2,1,0:T(8,128)}, u32[]{:S(2)}) %copy-start.2) | copy-done | bytes 1048600
  3.8 0.0 copy-start.3
  3.8 0.9 %copy-done.3 = bf16[2,256,256]{2,1,0:T(8,128)(2,1)S(1)} copy-done((bf16[2,256,256]{2,1,0:T(8,128)(2,1)S(1)}, bf16[2,256,256]{2,1,0:T(8,128)(2,1)}, u32[]{:S(2)}) %copy-start.3) | copy-done | bytes 262168
  4.8 0.0 copy-start.5
  4.8 0.8 %copy-done.5 = bf16[2,128,128]{2,1,0:T(8,128)(2,1)S(1)} copy-done((bf16[2,128,128]{2,1,0:T(8,128)(2,1)S(1)}, bf16[2,128,128]{2,1,0:T(8,128)(2,1)}, u32[]{:S(2)}) %copy-start.5) | copy-done | bytes 65560
  5.6 0.0 copy-start.6
  5.6 0.9 %copy-done.6 = bf16[2,256,256]{2,1,0:T(8,128)(2,1)S(1)} copy-done((bf16[2,256,256]{2,1,0:T(8,128)(2,1)S(1)}, bf16[2,256,256]{2,1,0:T(8,128)(2,1)}, u32[]{:S(2)}) %copy-start.6) | copy-done | bytes 262168
  6.5 0.0 copy-start.8
  6.5 0.8 %copy-done.8 = f32[2,64,128]{2,1,0:T(8,128)S(1)} copy-done((f32[2,64,128]{2,1,0:T(8,128)S(1)}, f32[2,64,128]{2,1,0:T(8,128)}, u32[]{:S(2)}) %copy-start.8) | copy-done | bytes 65560
  7.4 0.0 copy-start.14
  7.4 0.7 %copy-done.14 = bf16[2,16,128]{2,1,0:T(8,128)(2,1)S(1)} copy-done((bf16[2,16,128]{2,1,0:T(8,128)(2,1)S(1)}, bf16[2,16,128]{2,1,0:T(8,128)(2,1)}, u32[]{:S(2)}) %copy-start.14) | copy-done | bytes 8216
  8.1 0.0 copy-start.7
  8.1 0.0 copy-start.11
  8.1 0.0 copy-start.17
  8.1 0.0 copy-start.1
  8.1 0.0 copy-start.4
  8.1 5.9 %forward.1 = (f32[32,64,128]{2,1,0:T(8,128)S(1)}, f32[16,8,128]{2,1,0:T(8,128)S(1)}) custom-call(f32[32,64,128]{2,1,0:T(8,128)S(1)} %copy-done.2, f32[2,64,128]{2,1,0:T(8,128)S(1)} %copy-done.8, bf16[2,256,256]{2,1,0:T(8,128)(2,1)S(1)} %copy-done.6, bf16[2,256,256]{2,1,0:T(8,128)(2,1)S(1)} %copy-done.3, bf16[2,128,128]{2,1,0:T(8,128)(2,1)S(1)} %copy-done.5, ...), custom_call_target="tpu_custom_call" | custom-call | tf_op jit(solution)/shard_map/forward/pallas_call | solution.py:541
  14.0 0.0 copy-done.7
  14.0 0.0 copy-done.11
  14.0 0.0 copy-done.17
  14.0 0.0 copy-start.9
  14.0 0.0 copy-start.10
  14.0 0.0 copy-start.12
  14.0 0.0 copy-start.15
  14.0 0.0 copy-start.16
  14.1 17.8 %exchange.1 = (f32[16,8,128]{2,1,0:T(8,128)S(1)}, f32[16,8,128]{2,1,0:T(8,128)S(1)}) custom-call(f32[16,8,128]{2,1,0:T(8,128)S(1)} %get-tuple-element.7.msg, f32[16,8,128]{2,1,0:T(8,128)S(1)} %copy-done.11, f32[3,64,128]{2,1,0:T(8,128)S(1)} %copy-done.7, f32[8,128]{1,0:T(8,128)S(1)} %copy-done.17), custom_call_target="tpu_custom_call" | custom-call | tf_op jit(solution)/shard_map/exchange/pallas_call | solution.py:562
  31.9 0.0 copy-done.1
  31.9 0.0 copy-done.4
  31.9 0.0 copy-done.9
  31.9 0.0 copy-done.10
  31.9 0.0 copy-done.12
  31.9 0.0 copy-done.15
  31.9 0.0 copy-done.16
  31.9 5.4 %inverse.1 = (f32[32,64,128]{2,1,0:T(8,128)}, f32[32,64,128]{2,1,0:T(8,128)}) custom-call(f32[32,64,128]{2,1,0:T(8,128)S(1)} %get-tuple-element.6.base, f32[16,8,128]{2,1,0:T(8,128)S(1)} %get-tuple-element.8.faces, f32[16,8,128]{2,1,0:T(8,128)S(1)} %get-tuple-element.9.rest, f32[8,128]{1,0:T(8,128)S(1)} %copy-done.16, f32[8,128]{1,0:T(8,128)S(1)} %copy-done.15, ...), custom_call_target="tpu_custom_call" | custom-call | tf_op jit(solution)/shard_map/inverse/pallas_call | solution.py:571
Async XLA Ops:
  0.6 0.7 %copy-start.13 = (bf16[2,16,256]{2,1,0:T(8,128)(2,1)S(1)}, bf16[2,16,256]{2,1,0:T(8,128)(2,1)}, u32[]{:S(2)}) copy-start(bf16[2,16,256]{2,1,0:T(8,128)(2,1)} %constant.33.clone.ur_hbm) | copy-start | bytes 49156
  1.4 1.2 %copy-start = (f32[32,64,128]{2,1,0:T(8,128)S(1)}, f32[32,64,128]{2,1,0:T(8,128)}, u32[]{:S(2)}) copy-start(f32[32,64,128]{2,1,0:T(8,128)} %constant.35.clone.inv_hbm.inv) | copy-start | bytes 3145732
  2.6 1.2 %copy-start.2 = (f32[32,64,128]{2,1,0:T(8,128)S(1)}, f32[32,64,128]{2,1,0:T(8,128)}, u32[]{:S(2)}) copy-start(f32[32,64,128]{2,1,0:T(8,128)} %charge_hbm.1) | copy-start | bytes 3145732
  3.8 0.9 %copy-start.3 = (bf16[2,256,256]{2,1,0:T(8,128)(2,1)S(1)}, bf16[2,256,256]{2,1,0:T(8,128)(2,1)}, u32[]{:S(2)}) copy-start(bf16[2,256,256]{2,1,0:T(8,128)(2,1)} %constant.31.clone.x_hbm.x) | copy-start | bytes 786436
  4.8 0.8 %copy-start.5 = (bf16[2,128,128]{2,1,0:T(8,128)(2,1)S(1)}, bf16[2,128,128]{2,1,0:T(8,128)(2,1)}, u32[]{:S(2)}) copy-start(bf16[2,128,128]{2,1,0:T(8,128)(2,1)} %constant.32.clone.y_hbm.y) | copy-start | bytes 196612
  5.6 0.9 %copy-start.6 = (bf16[2,256,256]{2,1,0:T(8,128)(2,1)S(1)}, bf16[2,256,256]{2,1,0:T(8,128)(2,1)}, u32[]{:S(2)}) copy-start(bf16[2,256,256]{2,1,0:T(8,128)(2,1)} %constant.30.clone.z_hbm) | copy-start | bytes 786436
  6.5 0.8 %copy-start.8 = (f32[2,64,128]{2,1,0:T(8,128)S(1)}, f32[2,64,128]{2,1,0:T(8,128)}, u32[]{:S(2)}) copy-start(f32[2,64,128]{2,1,0:T(8,128)} %surface_hbm.1) | copy-start | bytes 196612
  7.4 0.7 %copy-start.14 = (bf16[2,16,128]{2,1,0:T(8,128)(2,1)S(1)}, bf16[2,16,128]{2,1,0:T(8,128)(2,1)}, u32[]{:S(2)}) copy-start(bf16[2,16,128]{2,1,0:T(8,128)(2,1)} %constant.34.clone.uc_hbm) | copy-start | bytes 24580
  8.1 5.9 %copy-start.7 = (f32[3,64,128]{2,1,0:T(8,128)S(1)}, f32[3,64,128]{2,1,0:T(8,128)}, u32[]{:S(2)}) copy-start(f32[3,64,128]{2,1,0:T(8,128)} %constant.37.clone.pair_ref) | copy-start | bytes 294916
  8.1 5.9 %copy-start.11 = (f32[16,8,128]{2,1,0:T(8,128)S(1)}, f32[16,8,128]{2,1,0:T(8,128)}, u32[]{:S(2)}) copy-start(f32[16,8,128]{2,1,0:T(8,128)} %constant.36.clone.own_ref) | copy-start | bytes 196612
  8.1 5.9 %copy-start.17 = (f32[8,128]{1,0:T(8,128)S(1)}, f32[8,128]{1,0:T(8,128)}, u32[]{:S(2)}) copy-start(f32[8,128]{1,0:T(8,128)} %constant.38.clone.signs_ref) | copy-start | bytes 12292
  8.1 23.8 %copy-start.1 = (f32[32,64,128]{2,1,0:T(8,128)S(1)}, f32[32,64,128]{2,1,0:T(8,128)}, u32[]{:S(2)}) copy-start(f32[32,64,128]{2,1,0:T(8,128)} %constant.35.clone.inv_hbm.inv) | copy-start | bytes 3145732
  8.1 23.8 %copy-start.4 = (bf16[2,256,256]{2,1,0:T(8,128)(2,1)S(1)}, bf16[2,256,256]{2,1,0:T(8,128)(2,1)}, u32[]{:S(2)}) copy-start(bf16[2,256,256]{2,1,0:T(8,128)(2,1)} %constant.41.clone.z) | copy-start | bytes 786436
  14.0 17.9 %copy-start.9 = (f32[128,128]{1,0:T(8,128)S(1)}, f32[128,128]{1,0:T(8,128)}, u32[]{:S(2)}) copy-start(f32[128,128]{1,0:T(8,128)} %constant.44.clone.sin_x2) | copy-start | bytes 196612
  14.0 17.9 %copy-start.10 = (f32[128,128]{1,0:T(8,128)S(1)}, f32[128,128]{1,0:T(8,128)}, u32[]{:S(2)}) copy-start(f32[128,128]{1,0:T(8,128)} %constant.43.clone.sin_y) | copy-start | bytes 196612
  14.0 17.9 %copy-start.12 = (f32[32,32]{1,0:T(8,128)S(1)}, f32[32,32]{1,0:T(8,128)}, u32[]{:S(2)}) copy-start(f32[32,32]{1,0:T(8,128)} %constant.42.clone.cos) | copy-start | bytes 12292
  14.0 17.9 %copy-start.15 = (f32[8,128]{1,0:T(8,128)S(1)}, f32[8,128]{1,0:T(8,128)}, u32[]{:S(2)}) copy-start(f32[8,128]{1,0:T(8,128)} %constant.40.clone.right) | copy-start | bytes 12292
  14.0 17.9 %copy-start.16 = (f32[8,128]{1,0:T(8,128)S(1)}, f32[8,128]{1,0:T(8,128)}, u32[]{:S(2)}) copy-start(f32[8,128]{1,0:T(8,128)} %constant.39.clone.left) | copy-start | bytes 12292

commit v2 on v0

--- a/solution.py
+++ b/solution.py
@@ -154,21 +154,22 @@
     sx[0] = sy[0] = 0.0
     ex, ey = np.eye(WIDTH)[0], np.eye(HEIGHT)[0]
     t = {}
-    t["zf"] = halves(np.kron(cosines.T, np.eye(8)))
-    t["zi"] = halves(np.kron(cosines, np.eye(8)))
-    t["x"] = halves(np.kron(np.eye(4), sin_x))
-    t["y"] = halves(sin_y)
+    t["zf"] = np.stack(halves(np.kron(cosines.T, np.eye(8))))
+    t["zi"] = np.stack(halves(np.kron(cosines, np.eye(8))))
+    t["x"] = np.stack(halves(np.kron(np.eye(4), sin_x)))
+    t["y"] = np.stack(halves(sin_y))
     plane = SCREEN + across[:, None] + along[None, :]
     t["plane"] = plane.astype(np.float32)
-    t["vert"] = [float(v) for v in vertical]
-    t["ur"] = halves(np.concatenate([np.kron(np.eye(4), (ux + ex)[None]), np.kron(np.eye(4), (ux * sx)[None])], 0))
+    ur = np.concatenate([np.kron(np.eye(4), (ux + ex)[None]), np.kron(np.eye(4), (ux * sx)[None]), np.zeros((8, 4 * WIDTH))], 0)
+    t["ur"] = np.stack(halves(ur))
     uc = np.zeros((16, HEIGHT))
     uc[0], uc[1], uc[2] = uy + ey, uy * sy, ey
-    t["uc"] = halves(uc)
+    t["uc"] = np.stack(halves(uc))
     spec = plane[None] + vertical[:, None, None]
     inner = np.zeros((WIDTH, HEIGHT))
     inner[1:, 1:] = 1.0
     inv = inner / spec
+    t["inv"] = np.where(inner > 0, inv, 1.0).astype(np.float32)
     row_near = np.einsum("a,kab->kb", ux * ux, inv)
     row_far = np.einsum("a,kab->kb", ux * ux * sx, inv)
     col_near = np.einsum("b,kab->ka", uy * uy, inv)
@@ -238,55 +239,6 @@
     return jnp.concatenate(parts, 1)
 
 
-def forward_kernel(vert, charge, surface, zh, zl, xh, xl, yh, yl, urh, url, uch, ucl, plane, base, msg, work):
-    ztab, xtab, ytab = (zh[...], zl[...]), (xh[...], xl[...]), (yh[...], yl[...])
-    for t in range(WIDTH // 16):
-        sides = []
-        for h in range(2):
-            at = pl.ds(16 * t + 8 * h, 8)
-            block = charge[:, at, :]
-            block = jnp.concatenate(
-                [block[:1] + surface[0:1, at, :], block[1:-1], block[-1:] + surface[1:2, at, :]], 0
-            )
-            sides.append(block.reshape(DEPTH * 8, HEIGHT))
-        out = dot3(ztab, halved(pair_lanes(sides)))
-        for h in range(2):
-            side = out[:, HEIGHT * h:HEIGHT * (h + 1)]
-            side = dot3(halved(side), ytab)
-            work[:, 16 * t + 8 * h:16 * t + 8 * h + 8, :] = side.reshape(DEPTH, 8, HEIGHT)
-    inner = interior()
-    flat = plane[...]
-    lane = lane_ids((8, HEIGHT))
-    for t in range(DEPTH // 8):
-        sides = [work[8 * t + 4 * h:8 * t + 4 * h + 4].reshape(4 * WIDTH, HEIGHT) for h in range(2)]
-        out = dot3(xtab, halved(pair_lanes(sides)))
-        for h in range(2):
-            side = out[:, HEIGHT * h:HEIGHT * (h + 1)].reshape(4, WIDTH, HEIGHT)
-            full = []
-            corner = []
-            for s in range(4):
-                k = 8 * t + 4 * h + s
-                one = jnp.where(inner, side[s] / (flat + vert[k]), side[s])
-                base[k] = jnp.where(inner, one, 0.0)
-                full.append(one)
-                corner.append(one[0:1])
-            full = jnp.concatenate(full, 0)
-            parts = halved(full)
-            rows = dot3((urh[...], url[...]), parts)
-            own = jnp.concatenate(corner + [jnp.zeros((4, HEIGHT), F32)], 0)
-            rows = jnp.where(lane == 0, own, rows)
-            cols = dot3((uch[...], ucl[...]), parts, ((1,), (1,)))
-            first = lane_ids((1, 4 * WIDTH)) % WIDTH == 0
-            near = jnp.where(first, cols[2:3], cols[0:1])
-            far = jnp.where(first, 0.0, cols[1:2])
-            for g in range(2):
-                at = slice(HEIGHT * g, HEIGHT * (g + 1))
-                msg[4 * t + 2 * h + g] = jnp.concatenate(
-                    [rows[2 * g:2 * g + 2], rows[4 + 2 * g:6 + 2 * g], near[:, at], far[:, at], jnp.zeros((2, HEIGHT), F32)],
-                    0,
-                )
-
-
 def shift_x(n_gx, n_gy, field, by):
     cut = (by % n_gx) * n_gy
     return jnp.concatenate([field[cut:], field[:cut]], 0)
@@ -381,10 +333,24 @@
     return alpha + second * (1 + beta), -second * alpha
 
 
-def exchange_kernel(n_gx, n_gy, msg, own_ref, pair_ref, signs_ref, faces, rest, got, back, landed, sems):
+def face_kernel(
+    n_gx, n_gy,
+    charge_hbm, surface_hbm, z_hbm, x_hbm, y_hbm, ur_hbm, uc_hbm, inv_hbm, own_hbm, pair_hbm, signs_hbm,
+    base_hbm, faces,
+    charge, surface, z, x, y, ur, uc, inv, own_ref, pair_ref, signs_ref,
+    work, base, msg, got, back, landed, load_sems, store_sems, sems,
+):
     count = n_gx * n_gy
     gx, gy = lax.axis_index("gx"), lax.axis_index("gy")
     me = gx * n_gy + gy
+    pairs = [(z_hbm, z), (surface_hbm, surface)]
+    pairs += [(charge_hbm.at[:, pl.ds(16 * t, 16), :], charge.at[:, pl.ds(16 * t, 16), :]) for t in range(WIDTH // 16)]
+    pairs += [(y_hbm, y), (x_hbm, x), (ur_hbm, ur), (uc_hbm, uc)]
+    pairs += [(inv_hbm.at[pl.ds(8 * t, 8)], inv.at[pl.ds(8 * t, 8)]) for t in range(DEPTH // 8)]
+    pairs += [(own_hbm, own_ref), (pair_hbm, pair_ref), (signs_hbm, signs_ref)]
+    copies = [pltpu.make_async_copy(s, d, load_sems.at[n]) for n, (s, d) in enumerate(pairs)]
+    for copy in copies:
+        copy.start()
 
     def partner(off):
         to = lax.rem(me + off, count)
@@ -393,32 +359,95 @@
     barrier = pltpu.get_barrier_semaphore()
     for off in range(1, count):
         pl.semaphore_signal(barrier, inc=1, device_id=partner(off)[1], device_id_type=pl.DeviceIdType.MESH)
+    copies[0].wait()
+    copies[1].wait()
+    ztab = (z[0], z[1])
+    for t in range(WIDTH // 16):
+        copies[2 + t].wait()
+        sides = []
+        for h in range(2):
+            at = pl.ds(16 * t + 8 * h, 8)
+            block = charge[:, at, :]
+            block = jnp.concatenate(
+                [block[:1] + surface[0:1, at, :], block[1:-1], block[-1:] + surface[1:2, at, :]], 0
+            )
+            sides.append(block.reshape(DEPTH * 8, HEIGHT))
+        out = dot3(ztab, halved(pair_lanes(sides)))
+        if t == 0:
+            copies[6].wait()
+            ytab = (y[0], y[1])
+        for h in range(2):
+            side = out[:, HEIGHT * h:HEIGHT * (h + 1)]
+            side = dot3(halved(side), ytab)
+            work[:, 16 * t + 8 * h:16 * t + 8 * h + 8, :] = side.reshape(DEPTH, 8, HEIGHT)
+    for copy in copies[7:10]:
+        copy.wait()
+    xtab, utab, ctab = (x[0], x[1]), (ur[0], ur[1]), (uc[0], uc[1])
+    inner = interior()
+    lane = lane_ids((8, HEIGHT))
+    pl.semaphore_wait(barrier, count - 1)
+    stores = []
+    first = [
+        pltpu.make_async_remote_copy(
+            src_ref=msg.at[to],
+            dst_ref=got.at[me],
+            send_sem=sems.at[0, 0, to],
+            recv_sem=sems.at[0, 1, me],
+            device_id={"gx": to // n_gy, "gy": to % n_gy},
+            device_id_type=pl.DeviceIdType.MESH,
+        )
+        for to in range(count)
+    ]
+    for t in range(DEPTH // 8):
+        copies[10 + t].wait()
+        sides = [work[8 * t + 4 * h:8 * t + 4 * h + 4].reshape(4 * WIDTH, HEIGHT) for h in range(2)]
+        out = dot3(xtab, halved(pair_lanes(sides)))
+        for h in range(2):
+            side = out[:, HEIGHT * h:HEIGHT * (h + 1)].reshape(4, WIDTH, HEIGHT)
+            full = []
+            corner = []
+            for s in range(4):
+                k = 8 * t + 4 * h + s
+                one = side[s] * inv[k]
+                base[k] = jnp.where(inner, one, 0.0)
+                full.append(one)
+                corner.append(one[0:1])
+            full = jnp.concatenate(full, 0)
+            parts = halved(full)
+            rows = dot3(utab, parts)
+            own = jnp.concatenate(corner + [jnp.zeros((4, HEIGHT), F32)], 0)
+            rows = jnp.where(lane == 0, own, rows[:8])
+            cols = dot3(ctab, parts, ((1,), (1,)))
+            edge = lane_ids((1, 4 * WIDTH)) % WIDTH == 0
+            near = jnp.where(edge, cols[2:3], cols[0:1])
+            far = jnp.where(edge, 0.0, cols[1:2])
+            for g in range(2):
+                at = slice(HEIGHT * g, HEIGHT * (g + 1))
+                msg[4 * t + 2 * h + g] = jnp.concatenate(
+                    [rows[2 * g:2 * g + 2], rows[4 + 2 * g:6 + 2 * g], near[:, at], far[:, at], jnp.zeros((2, HEIGHT), F32)],
+                    0,
+                )
+        stores.append(
+            pltpu.make_async_copy(base.at[pl.ds(8 * t, 8)], base_hbm.at[pl.ds(8 * t, 8)], store_sems.at[t])
+        )
+        stores[-1].start()
+        for to in range(4 * t, 4 * t + 4):
+            pl.when(me != to)(first[to].start)
+    for copy in copies[14:]:
+        copy.wait()
     coef, table = owner_tables(own_ref[me], pair_ref[...], signs_ref[...])
-    pl.semaphore_wait(barrier, count - 1)
-
-    def spread(source, target, which):
-        copies = []
-        for off in range(1, count):
-            to, device = partner(off)
-            copies.append(
-                pltpu.make_async_remote_copy(
-                    src_ref=source.at[to],
-                    dst_ref=target.at[me],
-                    send_sem=sems.at[which, 0, off],
-                    recv_sem=sems.at[which, 1, off],
-                    device_id=device,
-                    device_id_type=pl.DeviceIdType.MESH,
-                )
-            )
-            copies[-1].start()
-        target[me] = source[me]
-        return copies
-
-    first = spread(msg, got, 0)
-    for copy in first:
-        copy.wait_recv()
-    fields = [got[:, f, :] for f in range(6)]
-    r = start_modes(n_gx, n_gy, fields)
+    got[me] = msg[me]
+    for source in range(count):
+        arrival = pltpu.make_async_remote_copy(
+            src_ref=msg.at[source],
+            dst_ref=got.at[source],
+            send_sem=sems.at[0, 0, source],
+            recv_sem=sems.at[0, 1, source],
+            device_id={"gx": source // n_gy, "gy": source % n_gy},
+            device_id_type=pl.DeviceIdType.MESH,
+        )
+        pl.when(me != source)(arrival.wait_recv)
+    r = start_modes(n_gx, n_gy, [got[:, f, :] for f in range(6)])
     w = schur_modes(n_gx, n_gy, coef, table, *r)
     v = schur_modes(n_gx, n_gy, coef, table, *w)
     for f, field in enumerate(face_fields(n_gx, n_gy, r)):
@@ -429,14 +458,32 @@
     back[:, 7, :] = v[0][:, HEIGHT:]
     back[:, 14, :] = v[1]
     sums = (inner_product(r, r), inner_product(r, w), inner_product(w, w), inner_product(w, v))
-    lane = lane_ids((count, HEIGHT))
-    back[:, 15, :] = sum(jnp.where(lane == s, value, 0.0) for s, value in enumerate(sums))
-    second = spread(back, landed, 1)
+    lanes = lane_ids((count, HEIGHT))
+    back[:, 15, :] = sum(jnp.where(lanes == s, value, 0.0) for s, value in enumerate(sums))
+    second = []
+    for off in range(1, count):
+        to, device = partner(off)
+        second.append(
+            pltpu.make_async_remote_copy(
+                src_ref=back.at[to],
+                dst_ref=landed.at[me],
+                send_sem=sems.at[1, 0, off],
+                recv_sem=sems.at[1, 1, off],
+                device_id=device,
+                device_id_type=pl.DeviceIdType.MESH,
+            )
+        )
+        second[-1].start()
+    landed[me] = back[me]
+    for copy in stores:
+        copy.wait()
+    for to in range(count):
+        pl.when(me != to)(first[to].wait_send)
     for copy in second:
         copy.wait_recv()
-    for copy in first + second:
+    faces[...] = combine(landed[...])
+    for copy in second:
         copy.wait_send()
-    faces[...], rest[...] = combine(landed[...])
 
 
 def combine(landed):
@@ -444,12 +491,9 @@
     total = jnp.sum(far[:, 7:8, :], 0)
     lane = lane_ids((1, HEIGHT))
     c0, c1 = steps([jnp.sum(jnp.where(lane == s, total, 0.0)) for s in range(4)])
-    faces = c0 * near + c1 * far
     lead = near - c0 * far
-    rest = jnp.concatenate(
-        [lead[:, 0:2] - c1 * near[:, 6:8], lead[:, 4:5] - c1 * far[:, 6:7], jnp.zeros_like(near[:, :5])], 1
-    )
-    return faces, rest
+    rest = [lead[:, 0:2] - c1 * near[:, 6:8], lead[:, 4:5] - c1 * far[:, 6:7], jnp.zeros_like(near[:, :5])]
+    return jnp.concatenate([c0 * near + c1 * far] + rest, 1)
 
 
 def stacked(left, right):
@@ -460,20 +504,33 @@
     return dot(lhs, rhs, ((0,), (0,)))
 
 
-def inverse_kernel(vert, base, faces, rest, left, right, zh, zl, xh, xl, yh, yl, plane, cos, sin_y, sin_x2, potential, residual, work):
-    ztab, xtab, ytab = (zh[...], zl[...]), (xh[...], xl[...]), (yh[...], yl[...])
-    inner = interior()
-    flat = plane[...]
+def inverse_kernel(
+    faces_hbm, base_hbm, x_hbm, y_hbm, z_hbm, inv_hbm, small_hbm, square_hbm, potential_hbm, residual_hbm,
+    faces, base, x, y, z, inv, small, square, potential, residual, work, load_sems, store_sems,
+):
+    pairs = [(faces_hbm, faces), (small_hbm, small), (x_hbm, x), (y_hbm, y)]
+    for t in range(DEPTH // 8):
+        at = pl.ds(8 * t, 8)
+        pairs += [(inv_hbm.at[at], inv.at[at]), (base_hbm.at[at], base.at[at])]
+    pairs += [(square_hbm, square), (z_hbm, z)]
+    copies = [pltpu.make_async_copy(s, d, load_sems.at[n]) for n, (s, d) in enumerate(pairs)]
+    for copy in copies:
+        copy.start()
+    for copy in copies[:4]:
+        copy.wait()
+    xtab, ytab = (x[0], x[1]), (y[0], y[1])
     lane = lane_ids((8, HEIGHT))
     sub = lax.broadcasted_iota(jnp.int32, (8, HEIGHT), 0)
-    const_left, const_right = left[...], right[...]
+    const_left, const_right = small[0:8], small[8:16]
     for t in range(DEPTH // 8):
+        copies[4 + 2 * t].wait()
+        copies[5 + 2 * t].wait()
         sides = []
         for h in range(2):
             blocks = []
             for g in range(2):
                 o = 4 * t + 2 * h + g
-                one = faces[o]
+                one = faces[o, :8]
                 lhs = jnp.where((sub >= 4) & (sub < 6) & (lane % WIDTH > 0), one, const_left)
                 up = jnp.concatenate([one[2:], one[:2]], 0)
                 rhs = jnp.where((sub < 4) & (lane > 0), one, const_right)
@@ -481,25 +538,19 @@
                 out = stacked(lhs, rhs)
                 for s in range(2):
                     k = 2 * o + s
-                    part = out[WIDTH * s:WIDTH * (s + 1)]
-                    part = jnp.where(inner, part / (flat + vert[k]), part)
-                    blocks.append(part + base[k])
+                    blocks.append(out[WIDTH * s:WIDTH * (s + 1)] * inv[k] + base[k])
             sides.append(jnp.concatenate(blocks, 0))
         out = dot3(xtab, halved(pair_lanes(sides)))
         for h in range(2):
             side = dot3(halved(out[:, HEIGHT * h:HEIGHT * (h + 1)]), ytab)
             work[8 * t + 4 * h:8 * t + 4 * h + 4] = side.reshape(4, WIDTH, HEIGHT)
-    for t in range(WIDTH // 16):
-        sides = [work[:, 16 * t + 8 * h:16 * t + 8 * h + 8, :].reshape(DEPTH * 8, HEIGHT) for h in range(2)]
-        out = dot3(ztab, halved(pair_lanes(sides)))
-        for h in range(2):
-            side = out[:, HEIGHT * h:HEIGHT * (h + 1)]
-            potential[:, 16 * t + 8 * h:16 * t + 8 * h + 8, :] = side.reshape(DEPTH, 8, HEIGHT)
+    copies[12].wait()
+    cosines = square[2, :DEPTH, :DEPTH]
     half = DEPTH // 2
-    rows = jnp.concatenate([rest[:, 0, :], rest[:, 1, :]], 0)
-    rows = dot_exact(cos[...], dot_exact(rows, sin_y[...]))
-    cols = dot_exact(rest[:, 2, :], sin_x2[...])
-    cols = dot_exact(cos[...], jnp.concatenate([cols[:, :WIDTH], cols[:, WIDTH:]], 0))
+    rows = jnp.concatenate([faces[:, 8, :], faces[:, 9, :]], 0)
+    rows = dot_exact(cosines, dot_exact(rows, square[0]))
+    cols = dot_exact(faces[:, 10, :], square[1])
+    cols = dot_exact(cosines, jnp.concatenate([cols[:, :WIDTH], cols[:, WIDTH:]], 0))
     cols = jnp.concatenate([cols[:half], cols[half:]], 1)
     cols = jnp.where(lane_ids((half, HEIGHT)) % WIDTH == 0, 0.0, cols)
     unit = jnp.where(lane == 0, 1.0, 0.0)
@@ -510,42 +561,65 @@
         out = stacked(lhs, rhs)
         residual[2 * o] = out[:WIDTH]
         residual[2 * o + 1] = out[WIDTH:]
+    stores = [pltpu.make_async_copy(residual, residual_hbm, store_sems.at[WIDTH // 16])]
+    stores[0].start()
+    copies[13].wait()
+    ztab = (z[0], z[1])
+    for t in range(WIDTH // 16):
+        sides = [work[:, 16 * t + 8 * h:16 * t + 8 * h + 8, :].reshape(DEPTH * 8, HEIGHT) for h in range(2)]
+        out = dot3(ztab, halved(pair_lanes(sides)))
+        for h in range(2):
+            side = out[:, HEIGHT * h:HEIGHT * (h + 1)]
+            potential[:, 16 * t + 8 * h:16 * t + 8 * h + 8, :] = side.reshape(DEPTH, 8, HEIGHT)
+        at = pl.ds(16 * t, 16)
+        stores.append(pltpu.make_async_copy(potential.at[:, at, :], potential_hbm.at[:, at, :], store_sems.at[t]))
+        stores[-1].start()
+    for copy in stores:
+        copy.wait()
 
 
 def on_device_modes(n_gx, n_gy, charge, surface_charge):
     t = host_tables()
     count = n_gx * n_gy
     block = jax.ShapeDtypeStruct(charge.shape, F32)
-    small = jax.ShapeDtypeStruct((count, 8, HEIGHT), F32)
-    params = dict(vmem_limit_bytes=48 * 1024 * 1024)
-    base, msg = pl.pallas_call(
-        functools.partial(forward_kernel, t["vert"]),
-        out_shape=(block, small),
-        scratch_shapes=[pltpu.VMEM(charge.shape, F32)],
-        compiler_params=pltpu.CompilerParams(**params),
-        name="forward",
-    )(charge, surface_charge, *t["zf"], *t["x"], *t["y"], *t["ur"], *t["uc"], t["plane"])
+    hbm = pl.BlockSpec(memory_space=pl.ANY)
+    vmem = pl.BlockSpec(memory_space=pltpu.VMEM)
+
+    def held(values):
+        return [pltpu.VMEM(value.shape, value.dtype) for value in values]
+
     pair = np.concatenate([t["pair"], t["plane"][None]], 0)
-    faces, rest = pl.pallas_call(
-        functools.partial(exchange_kernel, n_gx, n_gy),
-        out_shape=(small, small),
-        scratch_shapes=[
-            pltpu.VMEM((count, 8, HEIGHT), F32),
-            pltpu.VMEM((count, 16, HEIGHT), F32),
-            pltpu.VMEM((count, 16, HEIGHT), F32),
+    args = [charge, surface_charge, t["zf"], t["x"], t["y"], t["ur"], t["uc"], t["inv"], t["own"], pair, t["signs"]]
+    eight, sixteen = (count, 8, HEIGHT), (count, 16, HEIGHT)
+    base, faces = pl.pallas_call(
+        functools.partial(face_kernel, n_gx, n_gy),
+        out_shape=(block, jax.ShapeDtypeStruct(sixteen, F32)),
+        in_specs=[hbm] * len(args),
+        out_specs=(hbm, vmem),
+        scratch_shapes=held(args)
+        + [pltpu.VMEM(shape, F32) for shape in (charge.shape, charge.shape, eight, eight, sixteen, sixteen)]
+        + [
+            pltpu.SemaphoreType.DMA((17,)),
+            pltpu.SemaphoreType.DMA((DEPTH // 8,)),
             pltpu.SemaphoreType.DMA((2, 2, count)),
         ],
-        in_specs=[pl.BlockSpec(memory_space=pltpu.VMEM)] * 4,
-        compiler_params=pltpu.CompilerParams(collective_id=0, has_side_effects=True, **params),
-        name="exchange",
-    )(msg, t["own"], pair, t["signs"])
+        compiler_params=pltpu.CompilerParams(collective_id=0, has_side_effects=True),
+        name="faces",
+    )(*args)
+    small = np.concatenate([t["left"], t["right"]], 0)
+    square = np.zeros((3, HEIGHT, HEIGHT), np.float32)
+    square[0], square[1], square[2, :DEPTH, :DEPTH] = t["sy"], t["sx2"], t["cos"]
+    args = [faces, base, t["x"], t["y"], t["zi"], t["inv"], small, square]
     return pl.pallas_call(
-        functools.partial(inverse_kernel, t["vert"]),
+        inverse_kernel,
         out_shape=(block, block),
-        scratch_shapes=[pltpu.VMEM(charge.shape, F32)],
-        compiler_params=pltpu.CompilerParams(**params),
+        in_specs=[hbm] * len(args),
+        out_specs=(hbm, hbm),
+        scratch_shapes=held(args)
+        + [pltpu.VMEM(charge.shape, F32)] * 3
+        + [pltpu.SemaphoreType.DMA((14,)), pltpu.SemaphoreType.DMA((WIDTH // 16 + 1,))],
         name="inverse",
-    )(base, faces, rest, t["left"], t["right"], *t["zi"], *t["x"], *t["y"], t["plane"], t["cos"], t["sy"], t["sx2"])
+    )(*args)
 
 
 def solution(mesh):

time: 37 us -> 27.9 us (0.75); the launches traced: 36.4 us -> 27.8 us
  local copies, waits for them, and re-layouts: 10.1 us -> 0 us
  Pallas kernels: 25.5 us -> 27.1 us
    unnamed x54 -> x0, local copies, waits for them, and re-layouts: 10.1 us -> none
    pallas_call x3 -> x2, Pallas kernels: 25.5 us -> 27.1 us  [the longest x1 19.8 us: on_device_modes(): pl.pallas_call(functools.partial(face_kernel, n_gx, n_gy), out_shape=(blo...]
where the time goes in v2:
time: 27.9 us; the launch traced here: 27.8 us
  Pallas kernels  27.1 us (97%)
  between operations  0.64 us (2%)
    pallas_call x1, Pallas kernels, on_device_modes(): pl.pallas_call(functools.partial(face_kernel, n_gx, n_gy), out_shape=(blo...  19.8 us
    pallas_call x1, Pallas kernels, on_device_modes(): pl.pallas_call(inverse_kernel, out_shape=(block, block), in_specs=[hbm] *...  7.35 us

profile of v2, /device:TPU:0, one launch (start us, length us, event | category | flops | bytes accessed | tf_op | source)
XLA Modules:
  0.0 27.8 jit_solution(8134840672447490462)
XLA Ops:
  0.6 19.8 %faces.1 = (f32[32,64,128]{2,1,0:T(8,128)}, f32[16,16,128]{2,1,0:T(8,128)}) custom-call(f32[32,64,128]{2,1,0:T(8,128)} %charge_hbm.1, f32[2,64,128]{2,1,0:T(8,128)} %surface_hbm.1, bf16[2,256,256]{2,1,0:T(8,128)(2,1)} %constant.24.clone.z_hbm, bf16[2,256,256]{2,1,0:T(8,128)(2,1)} %constant.25.clone.x_hbm, bf16[2,128,128]{2,1,0:T(8,128)(2,1)} %constant.26.clone.y_hbm, ...), custom_call_target="tpu_custom_call" | custom-call | tf_op jit(solution)/shard_map/faces/pallas_call | solution.py:594
  20.4 7.4 %inverse.1 = (f32[32,64,128]{2,1,0:T(8,128)}, f32[32,64,128]{2,1,0:T(8,128)}) custom-call(f32[16,16,128]{2,1,0:T(8,128)} %get-tuple-element.4.faces_hbm, f32[32,64,128]{2,1,0:T(8,128)} %get-tuple-element.5.base_hbm, bf16[2,256,256]{2,1,0:T(8,128)(2,1)} %constant.25.clone.x_hbm, bf16[2,128,128]{2,1,0:T(8,128)(2,1)} %constant.26.clone.y_hbm, ...), custom_call_target="tpu_custom_call" | custom-call | tf_op jit(solution)/shard_map/inverse/pallas_call | solution.py:613

commit v3 on v2

--- a/solution.py
+++ b/solution.py
@@ -154,17 +154,18 @@
     sx[0] = sy[0] = 0.0
     ex, ey = np.eye(WIDTH)[0], np.eye(HEIGHT)[0]
     t = {}
-    t["zf"] = np.stack(halves(np.kron(cosines.T, np.eye(8))))
-    t["zi"] = np.stack(halves(np.kron(cosines, np.eye(8))))
-    t["x"] = np.stack(halves(np.kron(np.eye(4), sin_x)))
-    t["y"] = np.stack(halves(sin_y))
+    t["zf"] = np.concatenate(halves(np.kron(cosines.T, np.eye(8))))
+    t["zi"] = np.concatenate(halves(np.kron(cosines, np.eye(8))))
+    t["x"] = np.concatenate(halves(np.kron(np.eye(4), sin_x)))
+    y_both = np.concatenate(halves(sin_y), 1)
+    t["y"] = np.concatenate([y_both, y_both], 0)
     plane = SCREEN + across[:, None] + along[None, :]
     t["plane"] = plane.astype(np.float32)
     ur = np.concatenate([np.kron(np.eye(4), (ux + ex)[None]), np.kron(np.eye(4), (ux * sx)[None]), np.zeros((8, 4 * WIDTH))], 0)
-    t["ur"] = np.stack(halves(ur))
+    t["ur"] = np.concatenate(halves(ur))
     uc = np.zeros((16, HEIGHT))
     uc[0], uc[1], uc[2] = uy + ey, uy * sy, ey
-    t["uc"] = np.stack(halves(uc))
+    t["uc"] = np.concatenate(halves(uc))
     spec = plane[None] + vertical[:, None, None]
     inner = np.zeros((WIDTH, HEIGHT))
     inner[1:, 1:] = 1.0
@@ -216,8 +217,16 @@
     return lax.dot_general(a, b, (dims, ((), ())), preferred_element_type=F32)
 
 
-def dot3(a, b, dims=((1,), (0,))):
-    return dot(a[0], b[0], dims) + (dot(a[0], b[1], dims) + dot(a[1], b[0], dims))
+def dot_table(table, b, dims=((1,), (0,))):
+    count = table.shape[0] // 2
+    both = dot(table, b[0], dims)
+    return both[:count] + (both[count:] + dot(table[:count], b[1], dims))
+
+
+def dot_packed(x, table):
+    out = dot(jnp.concatenate(halved(x), 1), table)
+    half = out.shape[1] // 2
+    return out[:, :half] + out[:, half:]
 
 
 def dot_exact(a, b, dims=((1,), (0,))):
@@ -264,8 +273,11 @@
     sx = functools.partial(shift_x, n_gx, n_gy)
     sy = functools.partial(shift_y, n_gx, n_gy)
     count = n_gx * n_gy
-    across = dot_exact(jnp.concatenate([col, col * col_sign], 0), table)
-    along = dot_exact(jnp.concatenate([row, row * row_sign], 0), table, ((1,), (1,)))
+    across = jnp.concatenate(halved(jnp.concatenate([col, col * col_sign], 0)), 1)
+    across = dot(across, table[0]) + dot(across, table[1])
+    along = dot(jnp.concatenate(halved(jnp.concatenate([row, row * row_sign], 0)), 0), table[2])
+    along = along[:2 * count] + along[2 * count:]
+    along = along[:, :HEIGHT] + along[:, HEIGHT:]
     v = across[:count] + sx(across[count:], -1)
     w = along[:count] + sy(along[count:], -1)
     row_out = row_coef * row - row_far * (sx(row, 1) + sx(row, -1)) - v - row_sign * sy(v, 1)
@@ -280,14 +292,23 @@
     return row_out, col_out
 
 
-def owner_tables(own, pair, signs):
+def owner_tables(own, pair, turned, signs):
     inner = interior()
-    parts = []
+    blank = jnp.zeros((WIDTH, HEIGHT), F32)
+    lane = lane_ids((HEIGHT, HEIGHT))
+    inside = (lane % WIDTH > 0) & (lax.broadcasted_iota(jnp.int32, (HEIGHT, HEIGHT), 0) > 0)
+    parts, other = [], []
     for s in range(2):
-        one = jnp.where(inner, pair[0] / (pair[2] + own[6 + s:7 + s]), pair[1])
-        parts.append(one)
-    blank = jnp.zeros((WIDTH, HEIGHT), F32)
-    table = jnp.concatenate([pair_lanes([parts[0], blank]), pair_lanes([blank, parts[1]])], 0)
+        vert = own[6 + s:7 + s]
+        parts.append(jnp.where(inner, pair[0] / (pair[2] + vert), pair[1]))
+        one = jnp.where(inside, turned[0] / (turned[2] + vert), turned[1])
+        other.append(jnp.where((lane < WIDTH) == (s == 0), one, 0.0))
+    high, low = halved(jnp.concatenate([pair_lanes([parts[0], blank]), pair_lanes([blank, parts[1]])], 0))
+    table = (
+        jnp.concatenate([high, high], 0),
+        jnp.concatenate([low, low], 0),
+        jnp.concatenate(halved(jnp.concatenate(other, 0)), 1),
+    )
     coef = (
         pair_lanes([own[0:1], own[1:2]]),
         pair_lanes([own[2:3], own[3:4]]),
@@ -311,7 +332,8 @@
     lane = lane_ids(first[1].shape)
     cols = jnp.where(lane % WIDTH == 0, 0.0, first[1] * second[1])
     rows = first[0] * second[0]
-    return jnp.sum(rows[:, :HEIGHT] + rows[:, HEIGHT:] + cols)
+    down = jnp.sum(rows[:, :HEIGHT] + rows[:, HEIGHT:] + cols, 0, keepdims=True)
+    return jnp.sum(down, 1, keepdims=True)
 
 
 def face_fields(n_gx, n_gy, pair):
@@ -335,9 +357,9 @@
 
 def face_kernel(
     n_gx, n_gy,
-    charge_hbm, surface_hbm, z_hbm, x_hbm, y_hbm, ur_hbm, uc_hbm, inv_hbm, own_hbm, pair_hbm, signs_hbm,
+    charge_hbm, surface_hbm, z_hbm, x_hbm, y_hbm, ur_hbm, uc_hbm, inv_hbm, own_hbm, pair_hbm, turned_hbm, signs_hbm,
     base_hbm, faces,
-    charge, surface, z, x, y, ur, uc, inv, own_ref, pair_ref, signs_ref,
+    charge, surface, z, x, y, ur, uc, inv, own_ref, pair_ref, turned_ref, signs_ref,
     work, base, msg, got, back, landed, load_sems, store_sems, sems,
 ):
     count = n_gx * n_gy
@@ -347,21 +369,23 @@
     pairs += [(charge_hbm.at[:, pl.ds(16 * t, 16), :], charge.at[:, pl.ds(16 * t, 16), :]) for t in range(WIDTH // 16)]
     pairs += [(y_hbm, y), (x_hbm, x), (ur_hbm, ur), (uc_hbm, uc)]
     pairs += [(inv_hbm.at[pl.ds(8 * t, 8)], inv.at[pl.ds(8 * t, 8)]) for t in range(DEPTH // 8)]
-    pairs += [(own_hbm, own_ref), (pair_hbm, pair_ref), (signs_hbm, signs_ref)]
+    pairs += [(own_hbm, own_ref), (pair_hbm, pair_ref), (turned_hbm, turned_ref), (signs_hbm, signs_ref)]
     copies = [pltpu.make_async_copy(s, d, load_sems.at[n]) for n, (s, d) in enumerate(pairs)]
     for copy in copies:
         copy.start()
 
     def partner(off):
-        to = lax.rem(me + off, count)
-        return to, {"gx": lax.div(to, n_gy), "gy": lax.rem(to, n_gy)}
+        to_x, to_y = gx + off // n_gy, gy + off % n_gy
+        to_x = jnp.where(to_x >= n_gx, to_x - n_gx, to_x)
+        to_y = jnp.where(to_y >= n_gy, to_y - n_gy, to_y)
+        return to_x * n_gy + to_y, {"gx": to_x, "gy": to_y}
 
     barrier = pltpu.get_barrier_semaphore()
     for off in range(1, count):
         pl.semaphore_signal(barrier, inc=1, device_id=partner(off)[1], device_id_type=pl.DeviceIdType.MESH)
     copies[0].wait()
     copies[1].wait()
-    ztab = (z[0], z[1])
+    ztab = z[...]
     for t in range(WIDTH // 16):
         copies[2 + t].wait()
         sides = []
@@ -372,17 +396,17 @@
                 [block[:1] + surface[0:1, at, :], block[1:-1], block[-1:] + surface[1:2, at, :]], 0
             )
             sides.append(block.reshape(DEPTH * 8, HEIGHT))
-        out = dot3(ztab, halved(pair_lanes(sides)))
+        out = dot_table(ztab, halved(pair_lanes(sides)))
         if t == 0:
             copies[6].wait()
-            ytab = (y[0], y[1])
+            ytab = y[...]
         for h in range(2):
             side = out[:, HEIGHT * h:HEIGHT * (h + 1)]
-            side = dot3(halved(side), ytab)
+            side = dot_packed(side, ytab)
             work[:, 16 * t + 8 * h:16 * t + 8 * h + 8, :] = side.reshape(DEPTH, 8, HEIGHT)
     for copy in copies[7:10]:
         copy.wait()
-    xtab, utab, ctab = (x[0], x[1]), (ur[0], ur[1]), (uc[0], uc[1])
+    xtab, utab, ctab = x[...], ur[...], uc[...]
     inner = interior()
     lane = lane_ids((8, HEIGHT))
     pl.semaphore_wait(barrier, count - 1)
@@ -401,7 +425,7 @@
     for t in range(DEPTH // 8):
         copies[10 + t].wait()
         sides = [work[8 * t + 4 * h:8 * t + 4 * h + 4].reshape(4 * WIDTH, HEIGHT) for h in range(2)]
-        out = dot3(xtab, halved(pair_lanes(sides)))
+        out = dot_table(xtab, halved(pair_lanes(sides)))
         for h in range(2):
             side = out[:, HEIGHT * h:HEIGHT * (h + 1)].reshape(4, WIDTH, HEIGHT)
             full = []
@@ -414,10 +438,10 @@
                 corner.append(one[0:1])
             full = jnp.concatenate(full, 0)
             parts = halved(full)
-            rows = dot3(utab, parts)
+            rows = dot_table(utab, parts)
             own = jnp.concatenate(corner + [jnp.zeros((4, HEIGHT), F32)], 0)
             rows = jnp.where(lane == 0, own, rows[:8])
-            cols = dot3(ctab, parts, ((1,), (1,)))
+            cols = dot_table(ctab, parts, ((1,), (1,)))
             edge = lane_ids((1, 4 * WIDTH)) % WIDTH == 0
             near = jnp.where(edge, cols[2:3], cols[0:1])
             far = jnp.where(edge, 0.0, cols[1:2])
@@ -435,7 +459,7 @@
             pl.when(me != to)(first[to].start)
     for copy in copies[14:]:
         copy.wait()
-    coef, table = owner_tables(own_ref[me], pair_ref[...], signs_ref[...])
+    coef, table = owner_tables(own_ref[me], pair_ref[...], turned_ref[...], signs_ref[...])
     got[me] = msg[me]
     for source in range(count):
         arrival = pltpu.make_async_remote_copy(
@@ -490,7 +514,8 @@
     near, far = landed[:, :8], landed[:, 8:]
     total = jnp.sum(far[:, 7:8, :], 0)
     lane = lane_ids((1, HEIGHT))
-    c0, c1 = steps([jnp.sum(jnp.where(lane == s, total, 0.0)) for s in range(4)])
+    c0, c1 = steps([jnp.sum(jnp.where(lane == s, total, 0.0), 1, keepdims=True) for s in range(4)])
+    c0, c1 = c0[None], c1[None]
     lead = near - c0 * far
     rest = [lead[:, 0:2] - c1 * near[:, 6:8], lead[:, 4:5] - c1 * far[:, 6:7], jnp.zeros_like(near[:, :5])]
     return jnp.concatenate([c0 * near + c1 * far] + rest, 1)
@@ -508,43 +533,19 @@
     faces_hbm, base_hbm, x_hbm, y_hbm, z_hbm, inv_hbm, small_hbm, square_hbm, potential_hbm, residual_hbm,
     faces, base, x, y, z, inv, small, square, potential, residual, work, load_sems, store_sems,
 ):
-    pairs = [(faces_hbm, faces), (small_hbm, small), (x_hbm, x), (y_hbm, y)]
+    pairs = [(faces_hbm, faces), (small_hbm, small), (square_hbm, square), (x_hbm, x), (y_hbm, y)]
     for t in range(DEPTH // 8):
         at = pl.ds(8 * t, 8)
         pairs += [(inv_hbm.at[at], inv.at[at]), (base_hbm.at[at], base.at[at])]
-    pairs += [(square_hbm, square), (z_hbm, z)]
+    pairs += [(z_hbm, z)]
     copies = [pltpu.make_async_copy(s, d, load_sems.at[n]) for n, (s, d) in enumerate(pairs)]
     for copy in copies:
         copy.start()
-    for copy in copies[:4]:
+    for copy in copies[:3]:
         copy.wait()
-    xtab, ytab = (x[0], x[1]), (y[0], y[1])
     lane = lane_ids((8, HEIGHT))
     sub = lax.broadcasted_iota(jnp.int32, (8, HEIGHT), 0)
     const_left, const_right = small[0:8], small[8:16]
-    for t in range(DEPTH // 8):
-        copies[4 + 2 * t].wait()
-        copies[5 + 2 * t].wait()
-        sides = []
-        for h in range(2):
-            blocks = []
-            for g in range(2):
-                o = 4 * t + 2 * h + g
-                one = faces[o, :8]
-                lhs = jnp.where((sub >= 4) & (sub < 6) & (lane % WIDTH > 0), one, const_left)
-                up = jnp.concatenate([one[2:], one[:2]], 0)
-                rhs = jnp.where((sub < 4) & (lane > 0), one, const_right)
-                rhs = jnp.where((sub >= 6) & (lane == 0), up, rhs)
-                out = stacked(lhs, rhs)
-                for s in range(2):
-                    k = 2 * o + s
-                    blocks.append(out[WIDTH * s:WIDTH * (s + 1)] * inv[k] + base[k])
-            sides.append(jnp.concatenate(blocks, 0))
-        out = dot3(xtab, halved(pair_lanes(sides)))
-        for h in range(2):
-            side = dot3(halved(out[:, HEIGHT * h:HEIGHT * (h + 1)]), ytab)
-            work[8 * t + 4 * h:8 * t + 4 * h + 4] = side.reshape(4, WIDTH, HEIGHT)
-    copies[12].wait()
     cosines = square[2, :DEPTH, :DEPTH]
     half = DEPTH // 2
     rows = jnp.concatenate([faces[:, 8, :], faces[:, 9, :]], 0)
@@ -563,11 +564,36 @@
         residual[2 * o + 1] = out[WIDTH:]
     stores = [pltpu.make_async_copy(residual, residual_hbm, store_sems.at[WIDTH // 16])]
     stores[0].start()
+    copies[3].wait()
+    copies[4].wait()
+    xtab, ytab = x[...], y[...]
+    for t in range(DEPTH // 8):
+        copies[5 + 2 * t].wait()
+        copies[6 + 2 * t].wait()
+        sides = []
+        for h in range(2):
+            blocks = []
+            for g in range(2):
+                o = 4 * t + 2 * h + g
+                one = faces[o, :8]
+                lhs = jnp.where((sub >= 4) & (sub < 6) & (lane % WIDTH > 0), one, const_left)
+                up = jnp.concatenate([one[2:], one[:2]], 0)
+                rhs = jnp.where((sub < 4) & (lane > 0), one, const_right)
+                rhs = jnp.where((sub >= 6) & (lane == 0), up, rhs)
+                out = stacked(lhs, rhs)
+                for s in range(2):
+                    k = 2 * o + s
+                    blocks.append(out[WIDTH * s:WIDTH * (s + 1)] * inv[k] + base[k])
+            sides.append(jnp.concatenate(blocks, 0))
+        out = dot_table(xtab, halved(pair_lanes(sides)))
+        for h in range(2):
+            side = dot_packed(out[:, HEIGHT * h:HEIGHT * (h + 1)], ytab)
+            work[8 * t + 4 * h:8 * t + 4 * h + 4] = side.reshape(4, WIDTH, HEIGHT)
     copies[13].wait()
-    ztab = (z[0], z[1])
+    ztab = z[...]
     for t in range(WIDTH // 16):
         sides = [work[:, 16 * t + 8 * h:16 * t + 8 * h + 8, :].reshape(DEPTH * 8, HEIGHT) for h in range(2)]
-        out = dot3(ztab, halved(pair_lanes(sides)))
+        out = dot_table(ztab, halved(pair_lanes(sides)))
         for h in range(2):
             side = out[:, HEIGHT * h:HEIGHT * (h + 1)]
             potential[:, 16 * t + 8 * h:16 * t + 8 * h + 8, :] = side.reshape(DEPTH, 8, HEIGHT)
@@ -589,7 +615,8 @@
         return [pltpu.VMEM(value.shape, value.dtype) for value in values]
 
     pair = np.concatenate([t["pair"], t["plane"][None]], 0)
-    args = [charge, surface_charge, t["zf"], t["x"], t["y"], t["ur"], t["uc"], t["inv"], t["own"], pair, t["signs"]]
+    turned = np.concatenate([np.swapaxes(pair, 1, 2)] * 2, 2)
+    args = [charge, surface_charge, t["zf"], t["x"], t["y"], t["ur"], t["uc"], t["inv"], t["own"], pair, turned, t["signs"]]
     eight, sixteen = (count, 8, HEIGHT), (count, 16, HEIGHT)
     base, faces = pl.pallas_call(
         functools.partial(face_kernel, n_gx, n_gy),
@@ -599,7 +626,7 @@
         scratch_shapes=held(args)
         + [pltpu.VMEM(shape, F32) for shape in (charge.shape, charge.shape, eight, eight, sixteen, sixteen)]
         + [
-            pltpu.SemaphoreType.DMA((17,)),
+            pltpu.SemaphoreType.DMA((18,)),
             pltpu.SemaphoreType.DMA((DEPTH // 8,)),
             pltpu.SemaphoreType.DMA((2, 2, count)),
         ],

time: 27.9 us -> 27 us (0.968)
  Pallas kernels: 27.1 us -> 26.2 us
    pallas_call x1, Pallas kernels: 7.35 us -> 6.79 us  [on_device_modes(): pl.pallas_call(inverse_kernel, out_shape=(block, block), in_specs=[hbm] *...]
    pallas_call x1, Pallas kernels: 19.8 us -> 19.5 us  [on_device_modes(): pl.pallas_call(functools.partial(face_kernel, n_gx, n_gy), out_shape=(blo...]
where the time goes in v3:
time: 27 us; the launch traced here: 26.9 us
  Pallas kernels  26.2 us (97%)
  between operations  0.64 us (2%)
    pallas_call x1, Pallas kernels, on_device_modes(): pl.pallas_call(functools.partial(face_kernel, n_gx, n_gy), out_shape=(blo...  19.5 us
    pallas_call x1, Pallas kernels, on_device_modes(): pl.pallas_call(inverse_kernel, out_shape=(block, block), in_specs=[hbm] *...  6.79 us

profile of v3, /device:TPU:0, one launch (start us, length us, event | category | flops | bytes accessed | tf_op | source)
XLA Modules:
  0.0 26.9 jit_solution(14052857621074740741)
XLA Ops:
  0.6 19.5 %faces.1 = (f32[32,64,128]{2,1,0:T(8,128)}, f32[16,16,128]{2,1,0:T(8,128)}) custom-call(f32[32,64,128]{2,1,0:T(8,128)} %charge_hbm.1, f32[2,64,128]{2,1,0:T(8,128)} %surface_hbm.1, bf16[512,256]{1,0:T(8,128)(2,1)} %constant.26.clone.z_hbm, bf16[512,256]{1,0:T(8,128)(2,1)} %constant.27.clone.x_hbm, bf16[256,256]{1,0:T(8,128)(2,1)} %constant.28.clone.y_hbm, ...), custom_call_target="tpu_custom_call" | custom-call | tf_op jit(solution)/shard_map/faces/pallas_call | solution.py:621
  20.1 6.8 %inverse.1 = (f32[32,64,128]{2,1,0:T(8,128)}, f32[32,64,128]{2,1,0:T(8,128)}) custom-call(f32[16,16,128]{2,1,0:T(8,128)} %get-tuple-element.4.faces_hbm, f32[32,64,128]{2,1,0:T(8,128)} %get-tuple-element.5.base_hbm, bf16[512,256]{1,0:T(8,128)(2,1)} %constant.27.clone.x_hbm, bf16[256,256]{1,0:T(8,128)(2,1)} %constant.28.clone.y_hbm, ...), custom_call_target="tpu_custom_call" | custom-call | tf_op jit(solution)/shard_map/inverse/pallas_call | solution.py:640

commit v4 on v3

--- a/solution.py
+++ b/solution.py
@@ -380,6 +380,22 @@
         to_y = jnp.where(to_y >= n_gy, to_y - n_gy, to_y)
         return to_x * n_gy + to_y, {"gx": to_x, "gy": to_y}
 
+    def send(source, target, which, off):
+        to, device = partner(off)
+        copy = pltpu.make_async_remote_copy(
+            src_ref=source.at[to],
+            dst_ref=target.at[me],
+            send_sem=sems.at[which, 0],
+            recv_sem=sems.at[which, 1],
+            device_id=device,
+            device_id_type=pl.DeviceIdType.MESH,
+        )
+        copy.start()
+
+    def all_done(buffer, sem):
+        whole = buffer.at[pl.ds(0, count - 1)]
+        pltpu.make_async_copy(whole, whole, sem).wait()
+
     barrier = pltpu.get_barrier_semaphore()
     for off in range(1, count):
         pl.semaphore_signal(barrier, inc=1, device_id=partner(off)[1], device_id_type=pl.DeviceIdType.MESH)
@@ -410,21 +426,12 @@
     inner = interior()
     lane = lane_ids((8, HEIGHT))
     pl.semaphore_wait(barrier, count - 1)
+    for copy in copies[10:14]:
+        copy.wait()
     stores = []
-    first = [
-        pltpu.make_async_remote_copy(
-            src_ref=msg.at[to],
-            dst_ref=got.at[me],
-            send_sem=sems.at[0, 0, to],
-            recv_sem=sems.at[0, 1, me],
-            device_id={"gx": to // n_gy, "gy": to % n_gy},
-            device_id_type=pl.DeviceIdType.MESH,
-        )
-        for to in range(count)
-    ]
-    for t in range(DEPTH // 8):
-        copies[10 + t].wait()
-        sides = [work[8 * t + 4 * h:8 * t + 4 * h + 4].reshape(4 * WIDTH, HEIGHT) for h in range(2)]
+    for step in range(1, n_gx + 1):
+        t = partner(n_gy * (step % n_gx))[1]["gx"]
+        sides = [work[pl.ds(8 * t + 4 * h, 4)].reshape(4 * WIDTH, HEIGHT) for h in range(2)]
         out = dot_table(xtab, halved(pair_lanes(sides)))
         for h in range(2):
             side = out[:, HEIGHT * h:HEIGHT * (h + 1)].reshape(4, WIDTH, HEIGHT)
@@ -448,29 +455,19 @@
             for g in range(2):
                 at = slice(HEIGHT * g, HEIGHT * (g + 1))
                 msg[4 * t + 2 * h + g] = jnp.concatenate(
-                    [rows[2 * g:2 * g + 2], rows[4 + 2 * g:6 + 2 * g], near[:, at], far[:, at], jnp.zeros((2, HEIGHT), F32)],
+                    [rows[2 * g:2 * g + 2], rows[4 + 2 * g:6 + 2 * g], near[:, at], far[:, at]],
                     0,
                 )
-        stores.append(
-            pltpu.make_async_copy(base.at[pl.ds(8 * t, 8)], base_hbm.at[pl.ds(8 * t, 8)], store_sems.at[t])
-        )
+        part = pl.ds(8 * t, 8)
+        stores.append(pltpu.make_async_copy(base.at[part], base_hbm.at[part], store_sems.at[step - 1]))
         stores[-1].start()
-        for to in range(4 * t, 4 * t + 4):
-            pl.when(me != to)(first[to].start)
+        for ahead in range(1 if step == n_gx else 0, n_gy):
+            send(msg, got, 0, n_gy * (step % n_gx) + ahead)
     for copy in copies[14:]:
         copy.wait()
     coef, table = owner_tables(own_ref[me], pair_ref[...], turned_ref[...], signs_ref[...])
     got[me] = msg[me]
-    for source in range(count):
-        arrival = pltpu.make_async_remote_copy(
-            src_ref=msg.at[source],
-            dst_ref=got.at[source],
-            send_sem=sems.at[0, 0, source],
-            recv_sem=sems.at[0, 1, source],
-            device_id={"gx": source // n_gy, "gy": source % n_gy},
-            device_id_type=pl.DeviceIdType.MESH,
-        )
-        pl.when(me != source)(arrival.wait_recv)
+    all_done(got, sems.at[0, 1])
     r = start_modes(n_gx, n_gy, [got[:, f, :] for f in range(6)])
     w = schur_modes(n_gx, n_gy, coef, table, *r)
     v = schur_modes(n_gx, n_gy, coef, table, *w)
@@ -484,30 +481,15 @@
     sums = (inner_product(r, r), inner_product(r, w), inner_product(w, w), inner_product(w, v))
     lanes = lane_ids((count, HEIGHT))
     back[:, 15, :] = sum(jnp.where(lanes == s, value, 0.0) for s, value in enumerate(sums))
-    second = []
     for off in range(1, count):
-        to, device = partner(off)
-        second.append(
-            pltpu.make_async_remote_copy(
-                src_ref=back.at[to],
-                dst_ref=landed.at[me],
-                send_sem=sems.at[1, 0, off],
-                recv_sem=sems.at[1, 1, off],
-                device_id=device,
-                device_id_type=pl.DeviceIdType.MESH,
-            )
-        )
-        second[-1].start()
+        send(back, landed, 1, off)
     landed[me] = back[me]
     for copy in stores:
         copy.wait()
-    for to in range(count):
-        pl.when(me != to)(first[to].wait_send)
-    for copy in second:
-        copy.wait_recv()
+    all_done(msg, sems.at[0, 0])
+    all_done(landed, sems.at[1, 1])
     faces[...] = combine(landed[...])
-    for copy in second:
-        copy.wait_send()
+    all_done(back, sems.at[1, 0])
 
 
 def combine(landed):
@@ -617,18 +599,18 @@
     pair = np.concatenate([t["pair"], t["plane"][None]], 0)
     turned = np.concatenate([np.swapaxes(pair, 1, 2)] * 2, 2)
     args = [charge, surface_charge, t["zf"], t["x"], t["y"], t["ur"], t["uc"], t["inv"], t["own"], pair, turned, t["signs"]]
-    eight, sixteen = (count, 8, HEIGHT), (count, 16, HEIGHT)
+    six, sixteen = (count, 6, HEIGHT), (count, 16, HEIGHT)
     base, faces = pl.pallas_call(
         functools.partial(face_kernel, n_gx, n_gy),
         out_shape=(block, jax.ShapeDtypeStruct(sixteen, F32)),
         in_specs=[hbm] * len(args),
         out_specs=(hbm, vmem),
         scratch_shapes=held(args)
-        + [pltpu.VMEM(shape, F32) for shape in (charge.shape, charge.shape, eight, eight, sixteen, sixteen)]
+        + [pltpu.VMEM(shape, F32) for shape in (charge.shape, charge.shape, six, six, sixteen, sixteen)]
         + [
             pltpu.SemaphoreType.DMA((18,)),
             pltpu.SemaphoreType.DMA((DEPTH // 8,)),
-            pltpu.SemaphoreType.DMA((2, 2, count)),
+            pltpu.SemaphoreType.DMA((2, 2)),
         ],
         compiler_params=pltpu.CompilerParams(collective_id=0, has_side_effects=True),
         name="faces",
@@ -650,9 +632,8 @@
 
 
 def solution(mesh):
-    count = mesh.shape["gx"] * mesh.shape["gy"]
     per_device = functools.partial(on_device_modes, mesh.shape["gx"], mesh.shape["gy"])
-    if 2 * count != DEPTH:
+    if (mesh.shape["gx"], mesh.shape["gy"]) != (4, 4):
         per_device = on_device
     in_specs = (P(None, ("slab", "gx"), "gy"), P(None, ("slab", "gx"), "gy"))
     out_specs = (P(None, ("slab", "gx"), "gy"), P(None, ("slab", "gx"), "gy"))

time: 27 us -> 25.8 us (0.956)
  Pallas kernels: 26.2 us -> 25 us
    pallas_call x1, Pallas kernels: 19.5 us -> 18.2 us  [on_device_modes(): pl.pallas_call(functools.partial(face_kernel, n_gx, n_gy), out_shape=(blo...]
where the time goes in v4:
time: 25.8 us; the launch traced here: 25.6 us
  Pallas kernels  25 us (97%)
  between operations  0.64 us (2%)
    pallas_call x1, Pallas kernels, on_device_modes(): pl.pallas_call(functools.partial(face_kernel, n_gx, n_gy), out_shape=(blo...  18.2 us
    pallas_call x1, Pallas kernels, on_device_modes(): pl.pallas_call(inverse_kernel, out_shape=(block, block), in_specs=[hbm] *...  6.79 us

profile of v4, /device:TPU:0, one launch (start us, length us, event | category | flops | bytes accessed | tf_op | source)
XLA Modules:
  0.0 25.6 jit_solution(1787649022449399114)
XLA Ops:
  0.6 18.2 %faces.1 = (f32[32,64,128]{2,1,0:T(8,128)}, f32[16,16,128]{2,1,0:T(8,128)}) custom-call(f32[32,64,128]{2,1,0:T(8,128)} %charge_hbm.1, f32[2,64,128]{2,1,0:T(8,128)} %surface_hbm.1, bf16[512,256]{1,0:T(8,128)(2,1)} %constant.26.clone.z_hbm, bf16[512,256]{1,0:T(8,128)(2,1)} %constant.27.clone.x_hbm, bf16[256,256]{1,0:T(8,128)(2,1)} %constant.28.clone.y_hbm, ...), custom_call_target="tpu_custom_call" | custom-call | tf_op jit(solution)/shard_map/faces/pallas_call | solution.py:603
  18.8 6.8 %inverse.1 = (f32[32,64,128]{2,1,0:T(8,128)}, f32[32,64,128]{2,1,0:T(8,128)}) custom-call(f32[16,16,128]{2,1,0:T(8,128)} %get-tuple-element.4.faces_hbm, f32[32,64,128]{2,1,0:T(8,128)} %get-tuple-element.5.base_hbm, bf16[512,256]{1,0:T(8,128)(2,1)} %constant.27.clone.x_hbm, bf16[256,256]{1,0:T(8,128)(2,1)} %constant.28.clone.y_hbm, ...), custom_call_target="tpu_custom_call" | custom-call | tf_op jit(solution)/shard_map/inverse/pallas_call | solution.py:622

commit v5 on v4

--- a/solution.py
+++ b/solution.py
@@ -202,9 +202,10 @@
     right[4], right[5] = uy + ey, uy * sy
     t["left"], t["right"] = left.astype(np.float32), right.astype(np.float32)
     split = np.concatenate([np.arange(0, DEPTH, 2), np.arange(1, DEPTH, 2)])
-    t["cos"] = cosines[split][:, split].astype(np.float32)
-    t["sy"] = sin_y.astype(np.float32)
-    t["sx2"] = np.kron(np.eye(2), sin_x).astype(np.float32)
+    pair_x = np.concatenate(halves(np.kron(np.eye(2), sin_x)), 1)
+    wide = np.zeros((DEPTH, 2 * HEIGHT))
+    wide[:, :DEPTH] = cosines[split][:, split]
+    t["square"] = np.concatenate([pair_x, pair_x] + list(halves(wide)), 0)
     return t
 
 
@@ -523,17 +524,21 @@
     copies = [pltpu.make_async_copy(s, d, load_sems.at[n]) for n, (s, d) in enumerate(pairs)]
     for copy in copies:
         copy.start()
-    for copy in copies[:3]:
+    for copy in copies[:5]:
         copy.wait()
     lane = lane_ids((8, HEIGHT))
     sub = lax.broadcasted_iota(jnp.int32, (8, HEIGHT), 0)
     const_left, const_right = small[0:8], small[8:16]
-    cosines = square[2, :DEPTH, :DEPTH]
+    xtab, ytab = x[...], y[...]
+    copies[5].wait()
+    copies[6].wait()
     half = DEPTH // 2
-    rows = jnp.concatenate([faces[:, 8, :], faces[:, 9, :]], 0)
-    rows = dot_exact(cosines, dot_exact(rows, square[0]))
-    cols = dot_exact(faces[:, 10, :], square[1])
-    cols = dot_exact(cosines, jnp.concatenate([cols[:, :WIDTH], cols[:, WIDTH:]], 0))
+    rows = dot_packed(jnp.concatenate([faces[:, 8, :], faces[:, 9, :]], 0), ytab)
+    cols = dot_packed(faces[:, 10, :], square[0:2 * HEIGHT])
+    cols = jnp.concatenate([cols[:, :WIDTH], cols[:, WIDTH:]], 0)
+    both = jnp.concatenate([rows, cols, jnp.zeros_like(cols)], 1)
+    both = dot_table(square[2 * HEIGHT:, :DEPTH], halved(both))
+    rows, cols = both[:, :HEIGHT], both[:, HEIGHT:HEIGHT + WIDTH]
     cols = jnp.concatenate([cols[:half], cols[half:]], 1)
     cols = jnp.where(lane_ids((half, HEIGHT)) % WIDTH == 0, 0.0, cols)
     unit = jnp.where(lane == 0, 1.0, 0.0)
@@ -544,14 +549,10 @@
         out = stacked(lhs, rhs)
         residual[2 * o] = out[:WIDTH]
         residual[2 * o + 1] = out[WIDTH:]
-    stores = [pltpu.make_async_copy(residual, residual_hbm, store_sems.at[WIDTH // 16])]
-    stores[0].start()
-    copies[3].wait()
-    copies[4].wait()
-    xtab, ytab = x[...], y[...]
     for t in range(DEPTH // 8):
-        copies[5 + 2 * t].wait()
-        copies[6 + 2 * t].wait()
+        if t > 0:
+            copies[5 + 2 * t].wait()
+            copies[6 + 2 * t].wait()
         sides = []
         for h in range(2):
             blocks = []
@@ -571,6 +572,9 @@
         for h in range(2):
             side = dot_packed(out[:, HEIGHT * h:HEIGHT * (h + 1)], ytab)
             work[8 * t + 4 * h:8 * t + 4 * h + 4] = side.reshape(4, WIDTH, HEIGHT)
+        if t == 0:
+            stores = [pltpu.make_async_copy(residual, residual_hbm, store_sems.at[WIDTH // 16])]
+            stores[0].start()
     copies[13].wait()
     ztab = z[...]
     for t in range(WIDTH // 16):
@@ -616,9 +620,7 @@
         name="faces",
     )(*args)
     small = np.concatenate([t["left"], t["right"]], 0)
-    square = np.zeros((3, HEIGHT, HEIGHT), np.float32)
-    square[0], square[1], square[2, :DEPTH, :DEPTH] = t["sy"], t["sx2"], t["cos"]
-    args = [faces, base, t["x"], t["y"], t["zi"], t["inv"], small, square]
+    args = [faces, base, t["x"], t["y"], t["zi"], t["inv"], small, t["square"]]
     return pl.pallas_call(
         inverse_kernel,
         out_shape=(block, block),

time: 25.8 us -> 25.5 us (0.988)
  Pallas kernels: 25 us -> 24.7 us
    pallas_call x1, Pallas kernels: 6.79 us -> 6.48 us  [on_device_modes(): pl.pallas_call(inverse_kernel, out_shape=(block, block), in_specs=[hbm] *...]
where the time goes in v5:
time: 25.5 us; the launch traced here: 25.3 us
  Pallas kernels  24.7 us (97%)
  between operations  0.64 us (3%)
    pallas_call x1, Pallas kernels, on_device_modes(): pl.pallas_call(functools.partial(face_kernel, n_gx, n_gy), out_shape=(blo...  18.2 us
    pallas_call x1, Pallas kernels, on_device_modes(): pl.pallas_call(inverse_kernel, out_shape=(block, block), in_specs=[hbm] *...  6.48 us

profile of v5, /device:TPU:0, one launch (start us, length us, event | category | flops | bytes accessed | tf_op | source)
XLA Modules:
  0.0 25.3 jit_solution(4796871573091795967)
XLA Ops:
  0.6 18.2 %faces.1 = (f32[32,64,128]{2,1,0:T(8,128)}, f32[16,16,128]{2,1,0:T(8,128)}) custom-call(f32[32,64,128]{2,1,0:T(8,128)} %charge_hbm.1, f32[2,64,128]{2,1,0:T(8,128)} %surface_hbm.1, bf16[512,256]{1,0:T(8,128)(2,1)} %constant.26.clone.z_hbm, bf16[512,256]{1,0:T(8,128)(2,1)} %constant.27.clone.x_hbm, bf16[256,256]{1,0:T(8,128)(2,1)} %constant.28.clone.y_hbm, ...), custom_call_target="tpu_custom_call" | custom-call | tf_op jit(solution)/shard_map/faces/pallas_call | solution.py:607
  18.8 6.5 %inverse.1 = (f32[32,64,128]{2,1,0:T(8,128)}, f32[32,64,128]{2,1,0:T(8,128)}) custom-call(f32[16,16,128]{2,1,0:T(8,128)} %get-tuple-element.4.faces_hbm, f32[32,64,128]{2,1,0:T(8,128)} %get-tuple-element.5.base_hbm, bf16[512,256]{1,0:T(8,128)(2,1)} %constant.27.clone.x_hbm, bf16[256,256]{1,0:T(8,128)(2,1)} %constant.28.clone.y_hbm, ...), custom_call_target="tpu_custom_call" | custom-call | tf_op jit(solution)/shard_map/inverse/pallas_call | solution.py:624

commit v6 on v5

--- a/solution.py
+++ b/solution.py
@@ -356,12 +356,14 @@
     return alpha + second * (1 + beta), -second * alpha
 
 
-def face_kernel(
+def slab_kernel(
     n_gx, n_gy,
     charge_hbm, surface_hbm, z_hbm, x_hbm, y_hbm, ur_hbm, uc_hbm, inv_hbm, own_hbm, pair_hbm, turned_hbm, signs_hbm,
-    base_hbm, faces,
+    zi_hbm, small_hbm, square_hbm,
+    potential_hbm, residual_hbm,
     charge, surface, z, x, y, ur, uc, inv, own_ref, pair_ref, turned_ref, signs_ref,
-    work, base, msg, got, back, landed, load_sems, store_sems, sems,
+    zi, small, square,
+    work, base, potential, residual, faces, msg, got, back, landed, load_sems, store_sems, sems,
 ):
     count = n_gx * n_gy
     gx, gy = lax.axis_index("gx"), lax.axis_index("gy")
@@ -371,6 +373,7 @@
     pairs += [(y_hbm, y), (x_hbm, x), (ur_hbm, ur), (uc_hbm, uc)]
     pairs += [(inv_hbm.at[pl.ds(8 * t, 8)], inv.at[pl.ds(8 * t, 8)]) for t in range(DEPTH // 8)]
     pairs += [(own_hbm, own_ref), (pair_hbm, pair_ref), (turned_hbm, turned_ref), (signs_hbm, signs_ref)]
+    pairs += [(zi_hbm, zi), (small_hbm, small), (square_hbm, square)]
     copies = [pltpu.make_async_copy(s, d, load_sems.at[n]) for n, (s, d) in enumerate(pairs)]
     for copy in copies:
         copy.start()
@@ -429,7 +432,6 @@
     pl.semaphore_wait(barrier, count - 1)
     for copy in copies[10:14]:
         copy.wait()
-    stores = []
     for step in range(1, n_gx + 1):
         t = partner(n_gy * (step % n_gx))[1]["gx"]
         sides = [work[pl.ds(8 * t + 4 * h, 4)].reshape(4 * WIDTH, HEIGHT) for h in range(2)]
@@ -459,9 +461,6 @@
                     [rows[2 * g:2 * g + 2], rows[4 + 2 * g:6 + 2 * g], near[:, at], far[:, at]],
                     0,
                 )
-        part = pl.ds(8 * t, 8)
-        stores.append(pltpu.make_async_copy(base.at[part], base_hbm.at[part], store_sems.at[step - 1]))
-        stores[-1].start()
         for ahead in range(1 if step == n_gx else 0, n_gy):
             send(msg, got, 0, n_gy * (step % n_gx) + ahead)
     for copy in copies[14:]:
@@ -485,11 +484,14 @@
     for off in range(1, count):
         send(back, landed, 1, off)
     landed[me] = back[me]
-    for copy in stores:
-        copy.wait()
     all_done(msg, sems.at[0, 0])
     all_done(landed, sems.at[1, 1])
     faces[...] = combine(landed[...])
+    stores = inverse(
+        faces, base, x, y, zi, inv, small, square, potential_hbm, residual_hbm, potential, residual, work, store_sems
+    )
+    for copy in stores:
+        copy.wait()
     all_done(back, sems.at[1, 0])
 
 
@@ -512,26 +514,13 @@
     return dot(lhs, rhs, ((0,), (0,)))
 
 
-def inverse_kernel(
-    faces_hbm, base_hbm, x_hbm, y_hbm, z_hbm, inv_hbm, small_hbm, square_hbm, potential_hbm, residual_hbm,
-    faces, base, x, y, z, inv, small, square, potential, residual, work, load_sems, store_sems,
+def inverse(
+    faces, base, x, y, z, inv, small, square, potential_hbm, residual_hbm, potential, residual, work, store_sems
 ):
-    pairs = [(faces_hbm, faces), (small_hbm, small), (square_hbm, square), (x_hbm, x), (y_hbm, y)]
-    for t in range(DEPTH // 8):
-        at = pl.ds(8 * t, 8)
-        pairs += [(inv_hbm.at[at], inv.at[at]), (base_hbm.at[at], base.at[at])]
-    pairs += [(z_hbm, z)]
-    copies = [pltpu.make_async_copy(s, d, load_sems.at[n]) for n, (s, d) in enumerate(pairs)]
-    for copy in copies:
-        copy.start()
-    for copy in copies[:5]:
-        copy.wait()
     lane = lane_ids((8, HEIGHT))
     sub = lax.broadcasted_iota(jnp.int32, (8, HEIGHT), 0)
     const_left, const_right = small[0:8], small[8:16]
     xtab, ytab = x[...], y[...]
-    copies[5].wait()
-    copies[6].wait()
     half = DEPTH // 2
     rows = dot_packed(jnp.concatenate([faces[:, 8, :], faces[:, 9, :]], 0), ytab)
     cols = dot_packed(faces[:, 10, :], square[0:2 * HEIGHT])
@@ -550,9 +539,6 @@
         residual[2 * o] = out[:WIDTH]
         residual[2 * o + 1] = out[WIDTH:]
     for t in range(DEPTH // 8):
-        if t > 0:
-            copies[5 + 2 * t].wait()
-            copies[6 + 2 * t].wait()
         sides = []
         for h in range(2):
             blocks = []
@@ -575,7 +561,6 @@
         if t == 0:
             stores = [pltpu.make_async_copy(residual, residual_hbm, store_sems.at[WIDTH // 16])]
             stores[0].start()
-    copies[13].wait()
     ztab = z[...]
     for t in range(WIDTH // 16):
         sides = [work[:, 16 * t + 8 * h:16 * t + 8 * h + 8, :].reshape(DEPTH * 8, HEIGHT) for h in range(2)]
@@ -586,8 +571,7 @@
         at = pl.ds(16 * t, 16)
         stores.append(pltpu.make_async_copy(potential.at[:, at, :], potential_hbm.at[:, at, :], store_sems.at[t]))
         stores[-1].start()
-    for copy in stores:
-        copy.wait()
+    return stores
 
 
 def on_device_modes(n_gx, n_gy, charge, surface_charge):
@@ -595,7 +579,6 @@
     count = n_gx * n_gy
     block = jax.ShapeDtypeStruct(charge.shape, F32)
     hbm = pl.BlockSpec(memory_space=pl.ANY)
-    vmem = pl.BlockSpec(memory_space=pltpu.VMEM)
 
     def held(values):
         return [pltpu.VMEM(value.shape, value.dtype) for value in values]
@@ -604,32 +587,22 @@
     turned = np.concatenate([np.swapaxes(pair, 1, 2)] * 2, 2)
     args = [charge, surface_charge, t["zf"], t["x"], t["y"], t["ur"], t["uc"], t["inv"], t["own"], pair, turned, t["signs"]]
     six, sixteen = (count, 6, HEIGHT), (count, 16, HEIGHT)
-    base, faces = pl.pallas_call(
-        functools.partial(face_kernel, n_gx, n_gy),
-        out_shape=(block, jax.ShapeDtypeStruct(sixteen, F32)),
-        in_specs=[hbm] * len(args),
-        out_specs=(hbm, vmem),
-        scratch_shapes=held(args)
-        + [pltpu.VMEM(shape, F32) for shape in (charge.shape, charge.shape, six, six, sixteen, sixteen)]
-        + [
-            pltpu.SemaphoreType.DMA((18,)),
-            pltpu.SemaphoreType.DMA((DEPTH // 8,)),
-            pltpu.SemaphoreType.DMA((2, 2)),
-        ],
-        compiler_params=pltpu.CompilerParams(collective_id=0, has_side_effects=True),
-        name="faces",
-    )(*args)
     small = np.concatenate([t["left"], t["right"]], 0)
-    args = [faces, base, t["x"], t["y"], t["zi"], t["inv"], small, t["square"]]
+    args += [t["zi"], small, t["square"]]
     return pl.pallas_call(
-        inverse_kernel,
+        functools.partial(slab_kernel, n_gx, n_gy),
         out_shape=(block, block),
         in_specs=[hbm] * len(args),
         out_specs=(hbm, hbm),
         scratch_shapes=held(args)
-        + [pltpu.VMEM(charge.shape, F32)] * 3
-        + [pltpu.SemaphoreType.DMA((14,)), pltpu.SemaphoreType.DMA((WIDTH // 16 + 1,))],
-        name="inverse",
+        + [pltpu.VMEM(shape, F32) for shape in [charge.shape] * 4 + [sixteen, six, six, sixteen, sixteen]]
+        + [
+            pltpu.SemaphoreType.DMA((21,)),
+            pltpu.SemaphoreType.DMA((WIDTH // 16 + 1,)),
+            pltpu.SemaphoreType.DMA((2, 2)),
+        ],
+        compiler_params=pltpu.CompilerParams(collective_id=0, has_side_effects=True),
+        name="slab",
     )(*args)
 
 

time: 25.5 us -> 26.4 us (1.035)
  local copies, waits for them, and re-layouts: 0 us -> 3.37 us
  Pallas kernels: 24.7 us -> 22.2 us
    unnamed x0 -> x4, local copies, waits for them, and re-layouts: none -> 3.37 us
    pallas_call x2 -> x1, Pallas kernels: 24.7 us -> 22.2 us  [on_device_modes(): pl.pallas_call(functools.partial(slab_kernel, n_gx, n_gy), out_shape=(blo...]
where the time goes in v6:
time: 26.4 us; the launch traced here: 26.2 us
  Pallas kernels  22.2 us (84%)
  local copies, waits for them, and re-layouts  3.37 us (13%)
  between operations  0.65 us (2%)
    pallas_call x1, Pallas kernels, on_device_modes(): pl.pallas_call(functools.partial(slab_kernel, n_gx, n_gy), out_shape=(blo...  22.2 us
    unnamed x4, local copies, waits for them, and re-layouts  3.37 us

profile of v6, /device:TPU:0, one launch (start us, length us, event | category | flops | bytes accessed | tf_op | source)
XLA Modules:
  0.0 26.2 jit_solution(11149034853649880178)
XLA Ops:
  0.6 22.2 %slab.1 = (f32[32,64,128]{2,1,0:T(8,128)}, f32[32,64,128]{2,1,0:T(8,128)}) custom-call(f32[32,64,128]{2,1,0:T(8,128)} %charge_hbm.1, f32[2,64,128]{2,1,0:T(8,128)} %surface_hbm.1, bf16[512,256]{1,0:T(8,128)(2,1)} %constant.26.clone.z_hbm, bf16[512,256]{1,0:T(8,128)(2,1)} %constant.27.clone.x_hbm, bf16[256,256]{1,0:T(8,128)(2,1)} %constant.28.clone.y_hbm, ...), custom_call_target="tpu_custom_call" | custom-call | tf_op jit(solution)/shard_map/slab/pallas_call | solution.py:592
  22.8 0.0 copy-start
  22.9 2.4 %copy.19 = f32[32,64,128]{2,1,0:T(8,128)} copy(f32[32,64,128]{2,1,0:T(8,128)} %get-tuple-element.4) | data formatting | bytes 2097152
  25.3 0.0 copy-done
  25.3 1.0 %copy.20 = f32[32,64,128]{2,1,0:T(8,128)} copy(f32[32,64,128]{2,1,0:T(8,128)S(1)} %copy-done) | data formatting | bytes 2097152
Async XLA Ops:
  22.8 2.4 %copy-start = (f32[32,64,128]{2,1,0:T(8,128)S(1)}, f32[32,64,128]{2,1,0:T(8,128)}, u32[]{:S(2)}) copy-start(f32[32,64,128]{2,1,0:T(8,128)} %get-tuple-element.5) | copy-start | bytes 3145732
